TPU v7x, 128 devices: a whole 4x4x4 slice. The times are simulated.
128 devices in a mesh: grp: 16 (over x, z), mem: 8 (over y, core).
Axes of the slice: x: 4, y: 4, z: 4, core: 2. Of those that a mesh axis runs over, the one named last changes fastest.
Arguments:
- hidden: bfloat16 [262144, 256], P(('grp', 'mem')), may hold values from -6 to 6
- initial: bfloat16 [262144, 256], P(('grp', 'mem')), may hold values from -6 to 6
- weight: bfloat16 [256, 256], replicated, may hold values from -0.375 to 0.375
- grp_vals: bfloat16 [28672, 128, 128], P(('grp', 'mem')), may hold values from -0.125 to 0.125
- grp_row: int32 [28672], P(('grp', 'mem')), may hold values from 0 to 15
- grp_col: int32 [28672], P(('grp', 'mem')), may hold values from 0 to 127
- bnd_vals: bfloat16 [14336, 128, 128], P(('grp', 'mem')), may hold values from -0.125 to 0.125
- bnd_src: int32 [14336], P(('grp', 'mem')), may hold values from 0 to 15
- bnd_dst: int32 [14336, 1], P(('grp', 'mem')), may hold values from 0 to 127; in each aligned block of 112 rows (0 to 111, 112 to 223, ...) at most 2 rows name the same one
- bnd_row: int32 [14336], P(('grp', 'mem')), may hold values from 0 to 15
- cotangent: bfloat16 [262144, 256], P(('grp', 'mem')), may hold values from -6 to 6
Outputs:
- output: bfloat16 [262144, 256], P(('grp', 'mem'))
- grad_weight: float32 [256, 256], replicated
- grad_hidden: bfloat16 [262144, 256], P(('grp', 'mem'))
Inputs may be any that keep to these rules, and one draw needn't show every extreme that they name: `bnd_dst`: among the boundary edge blocks of one device, at most 2 name any one device, and on some device exactly 2 name one device.
All inputs are finite; a program needn't handle non-finite values.
Results may differ from a plain program's by a relative error of at most 0.017.
Values may be sent and summed in bfloat16 or wider, within the bound.
A program may use at most 256 MiB of HBM per device.

v0:
```python
import math

import jax
import jax.numpy as jnp
from jax import lax
from jax.sharding import PartitionSpec as P


def per_device(
    hidden,
    initial,
    weight,
    grp_vals,
    grp_row,
    grp_col,
    bnd_vals,
    bnd_src,
    bnd_dst,
    bnd_row,
    cotangent,
):
    block_size = grp_vals.shape[1]
    features = hidden.shape[1]
    node_blocks = hidden.shape[0] // block_size
    devices = lax.axis_size(("grp", "mem"))
    boundary_count = bnd_vals.shape[0]
    capacity = max(2, 2 * boundary_count // devices)
    blocks = hidden.reshape(node_blocks, block_size, features)
    table = lax.all_gather(blocks, "mem", axis=0, tiled=True)
    picked = table[grp_col]
    messages = jnp.einsum("bij,bjf->bif", grp_vals, picked, preferred_element_type=jnp.float32)
    block_ids = jnp.arange(node_blocks, dtype=jnp.int32)
    summed = jnp.zeros((node_blocks, block_size, features), jnp.float32).at[grp_row].add(messages)
    partial_value = jnp.einsum(
        "bij,bjf->bif", bnd_vals, blocks[bnd_src], preferred_element_type=jnp.float32
    ).astype(jnp.bfloat16)
    target = bnd_dst[:, 0]
    hits = (target[:, None] == jnp.arange(devices, dtype=jnp.int32)[None, :]).astype(jnp.int32)
    earlier = jnp.cumsum(hits, axis=0) - hits
    place_in = jnp.sum(earlier * hits, axis=1)
    slot = target * capacity + place_in
    outgoing = (
        jnp.zeros((devices * capacity, block_size, features), jnp.bfloat16)
        .at[slot]
        .set(partial_value)
    )
    out_rows = jnp.full((devices * capacity,), -1, jnp.int32).at[slot].set(bnd_row)
    incoming, in_rows = (
        lax.all_to_all(
            outgoing.reshape(devices, capacity, block_size, features),
            ("grp", "mem"),
            split_axis=0,
            concat_axis=0,
            tiled=True,
        ),
        lax.all_to_all(
            out_rows.reshape(devices, capacity),
            ("grp", "mem"),
            split_axis=0,
            concat_axis=0,
            tiled=True,
        ),
    )
    incoming = incoming.reshape(devices * capacity, block_size, features)
    in_rows = in_rows.reshape(devices * capacity)
    recv_select = (in_rows[None, :] == block_ids[:, None]).astype(jnp.bfloat16)
    summed = summed + jnp.einsum(
        "rs,sif->rif", recv_select, incoming, preferred_element_type=jnp.float32
    )
    mixed = (0.9 * summed.reshape(-1, features) + 0.1 * initial.astype(jnp.float32)).astype(
        jnp.bfloat16
    )
    mix_weight = (
        0.5 * jnp.eye(features, dtype=jnp.float32) + 0.5 * weight.astype(jnp.float32)
    ).astype(jnp.bfloat16)
    pre = jnp.dot(mixed, mix_weight, preferred_element_type=jnp.float32)
    output = jax.nn.silu(pre).astype(jnp.bfloat16)
    sigmoid_pre = jax.nn.sigmoid(pre)
    grad_pre = (
        cotangent.astype(jnp.float32) * sigmoid_pre * (1.0 + pre * (1.0 - sigmoid_pre))
    ).astype(jnp.bfloat16)
    local_weight = lax.dot_general(
        mixed, grad_pre, (((0,), (0,)), ((), ())), preferred_element_type=jnp.float32
    )
    total_nodes = hidden.shape[0] * devices
    grad_weight = 0.5 * lax.psum(local_weight, ("grp", "mem")) / math.sqrt(total_nodes)
    grad_mixed = lax.dot_general(
        grad_pre, mix_weight, (((1,), (1,)), ((), ())), preferred_element_type=jnp.float32
    ).astype(jnp.bfloat16)
    grad_blocks = grad_mixed.reshape(node_blocks, block_size, features)
    transposed = jnp.einsum(
        "bji,bjf->bif", grp_vals, grad_blocks[grp_row], preferred_element_type=jnp.float32
    )
    start = jnp.int32(0)
    inside = (grp_col >= start) & (grp_col < start + node_blocks * lax.axis_size("mem"))
    local = jnp.where(inside, grp_col, node_blocks * lax.axis_size("mem"))
    term = (
        jnp.zeros((node_blocks * lax.axis_size("mem"), block_size, features), jnp.float32)
        .at[local]
        .add(transposed, mode="drop")
    )
    grad_table = lax.psum_scatter(
        (0.9 * term).astype(jnp.bfloat16), "mem", scatter_dimension=0, tiled=True
    )
    grad_hidden = grad_table.reshape(-1, features)
    return (output, grad_weight, grad_hidden)


def solution(mesh):
    return jax.shard_map(
        per_device,
        mesh=mesh,
        in_specs=(
            P(("grp", "mem"), None),
            P(("grp", "mem"), None),
            P(),
            P(("grp", "mem"), None, None),
            P(("grp", "mem")),
            P(("grp", "mem")),
            P(("grp", "mem"), None, None),
            P(("grp", "mem")),
            P(("grp", "mem"), None),
            P(("grp", "mem")),
            P(("grp", "mem"), None),
        ),
        out_specs=(P(("grp", "mem"), None), P(), P(("grp", "mem"), None)),
        check_vma=False,
    )
```

profile of v0, /device:TPU:1, one launch (start us, length us, event | category | flops | bytes accessed | tf_op | source)
XLA Modules:
  0.0 653.8 jit_solution(17323045345636502749)
XLA Ops:
  7.2 0.7 fusion.2
  7.9 0.2 reduce_window_sum.11
  8.1 0.8 select_reduce_fusion
  8.9 0.7 fusion.7
  9.6 1.1 scatter_custom_fusion
  10.6 0.8 all_to_all.9
  11.4 11.5 %all-to-all-start = ((s32[128,1,2]{2,1,0:T(1,128)}), s32[128,1,2]{2,1,0:T(1,128)S(1)}, u32[]{:S(2)}, u32[]{:S(2)}) async-start(s32[128,1,2]{2,1,0:T(1,128)} %bitcast.3), calls=%async_computation | async-start | bytes 131072 | tf_op jit(solution)/shard_map/all_to_all | solution.py:56
  22.9 0.0 all-gather.2.cloned.1.call-start
  23.0 0.7 all-gather.2.cloned.1.call-update
  23.6 0.7 compare_select_fusion.3
  24.3 7.6 %gather_fusion = bf16[112,128,256]{2,1,0:T(8,128)(2,1)} fusion(bf16[16,128,256]{2,1,0:T(8,128)(2,1)} %bitcast.41, s32[1024]{0:T(1024)S(1)} %pad_clamp_fusion.2), kind=kCustom, calls=%fused_computation | custom fusion | bytes 14680512 | tf_op jit(solution)/shard_map/gather | solution.py:35
  31.9 9.3 %convert_bitcast_fusion = bf16[112,128,256]{1,2,0:T(8,128)(2,1)} fusion(bf16[112,128,256]{2,1,0:T(8,128)(2,1)} %gather_fusion, bf16[112,128,128]{2,1,0:T(8,128)(2,1)} %param.17), kind=kOutput, calls=%fused_computation.10 | convolution fusion | flops 943194112 | bytes 18350080 | tf_op jit(solution)/shard_map/bij,bjf->bif/dot_general | solution.py:34
  41.2 10.2 %copy.29 = bf16[112,128,256]{2,1,0:T(8,128)(2,1)} copy(bf16[112,128,256]{1,2,0:T(8,128)(2,1)} %convert_bitcast_fusion) | data formatting | bytes 14680064 | tf_op jit(solution)/shard_map/convert_element_type | solution.py:36
  51.4 6.0 broadcast_in_dim.30
  57.4 21.0 %scatter_fusion = bf16[256,128,256]{2,1,0:T(8,128)(2,1)} fusion(bf16[256,128,256]{2,1,0:T(8,128)(2,1)} %broadcast_in_dim.30, s32[112]{0:T(128)S(1)} %fusion.7, bf16[112,128,256]{2,1,0:T(8,128)(2,1)} %copy.29), kind=kCustom, calls=%fused_computation.4 | custom fusion | bytes 22020544 | tf_op jit(solution)/shard_map/scatter | solution.py:45
  78.4 30.7 %copy.30 = bf16[128,2,128,256]{3,1,2,0:T(2,128)(2,1)} copy(bf16[128,2,128,256]{3,2,1,0:T(8,128)(2,1)} %bitcast.39) | data formatting | bytes 33554432 | tf_op jit(solution)/shard_map/reshape | solution.py:50
  109.1 10.3 %all-to-all-start.1 = ((bf16[128,2,128,256]{3,1,2,0:T(2,128)(2,1)}), bf16[128,2,128,256]{3,1,2,0:T(2,128)(2,1)}, u32[]{:S(2)}, u32[]{:S(2)}) async-start(bf16[128,2,128,256]{3,1,2,0:T(2,128)(2,1)} %copy.30), calls=%async_computation.1 | async-start | bytes 33554432 | tf_op jit(solution)/shard_map/all_to_all | solution.py:49
  119.4 0.2 all-reduce.2.cloned.1.call-start
  119.7 0.5 broadcast.76
  120.2 0.8 reduce.3
  121.0 0.1 eq.37
  121.2 0.0 all-gather.2.cloned.1.call-done
  121.2 12.6 %gather_fusion.1 = bf16[224,128,256]{2,1,0:T(8,128)(2,1)} fusion(bf16[128,128,256]{2,1,0:T(8,128)(2,1)} %all-gather.2.cloned.1.call-done, s32[1024]{0:T(1024)S(1)} %pad_clamp_fusion.1), kind=kCustom, calls=%fused_computation.1 | custom fusion | bytes 29361024 | tf_op jit(solution)/shard_map/gather | solution.py:30
  133.8 18.0 %convolution_bitcast_fusion.1 = f32[224,128,256]{1,2,0:T(8,128)} fusion(bf16[224,128,256]{2,1,0:T(8,128)(2,1)} %gather_fusion.1, bf16[224,128,128]{2,1,0:T(8,128)(2,1)} %param.14), kind=kOutput, calls=%fused_computation.9 | convolution fusion | flops 1879048192 | bytes 51380224 | tf_op jit(solution)/shard_map/bij,bjf->bif/dot_general | solution.py:31
  151.9 29.5 %copy.34 = f32[224,128,256]{2,1,0:T(8,128)} copy(f32[224,128,256]{1,2,0:T(8,128)} %convolution_bitcast_fusion.1) | data formatting | bytes 58720256 | tf_op jit(solution)/shard_map/bij,bjf->bif/dot_general | solution.py:31
  181.4 170.4 %all-to-all-done.1 = bf16[128,2,128,256]{3,1,2,0:T(2,128)(2,1)} async-done(((bf16[128,2,128,256]{3,1,2,0:T(2,128)(2,1)}), bf16[128,2,128,256]{3,1,2,0:T(2,128)(2,1)}, u32[]{:S(2)}, u32[]{:S(2)}) %all-to-all-start.1) | async-done | bytes 16777248 | tf_op jit(solution)/shard_map/all_to_all | solution.py:49
  351.8 14.4 %copy.31 = bf16[128,2,128,256]{3,1,0,2:T(2,128)(2,1)} copy(bf16[128,2,128,256]{3,1,2,0:T(2,128)(2,1)} %all-to-all-done.1) | data formatting | bytes 33554432 | tf_op jit(solution)/shard_map/all_to_all | solution.py:49
  366.2 24.8 %reshape.33 = bf16[256,128,256]{2,0,1:T(8,128)(2,1)} reshape(bf16[128,2,128,256]{3,1,0,2:T(2,128)(2,1)} %copy.31) | data formatting | bytes 33554432 | tf_op jit(solution)/shard_map/reshape | solution.py:64
  391.0 8.0 %fusion.4 = f32[16,128,256]{2,0,1:T(8,128)S(1)} fusion(bf16[256,128,256]{2,0,1:T(8,128)(2,1)} %reshape.33, s32[256]{0:T(256)S(1)} %eq.37), kind=kOutput, calls=%fused_computation.27 | convolution fusion | flops 268439552 | bytes 18875392 | tf_op jit(solution)/shard_map/rs,sif->rif/dot_general | solution.py:67
  399.1 1.2 copy.33
  400.3 42.2 %scatter_fusion.1 = f32[16,128,256]{2,1,0:T(8,128)S(1)} fusion(f32[16,128,256]{2,1,0:T(8,128)S(1)} %copy.33, s32[224]{0:T(256)S(1)} %compare_select_fusion.2, f32[224,128,256]{2,1,0:T(8,128)} %copy.34), kind=kCustom, calls=%fused_computation.5 | custom fusion | flops 7340032 | bytes 88081280 | tf_op jit(solution)/shard_map/scatter-add | solution.py:33
  442.5 0.2 broadcast_multiply_fusion
  442.7 0.4 fusion
  443.1 0.3 copy-done.1
  443.4 0.4 copy-done.4
  443.8 2.2 multiply_convert_fusion.1
  445.9 1.2 fusion.14
  447.1 0.5 convolution_convert_fusion
  447.6 0.3 reduce-scatter.2.cloned.1.call-start
  447.9 9.2 %gather_fusion.2 = bf16[224,128,256]{2,1,0:T(8,128)(2,1)} fusion(bf16[16,128,256]{2,1,0:T(8,128)(2,1)S(1)} %bitcast.38, s32[1024]{0:T(1024)S(1)} %pad_clamp_fusion), kind=kCustom, calls=%fused_computation.2 | custom fusion | bytes 29361024 | tf_op jit(solution)/shard_map/gather | solution.py:92
  457.1 18.1 %convolution_bitcast_fusion = f32[224,128,256]{1,2,0:T(8,128)} fusion(bf16[224,128,256]{2,1,0:T(8,128)(2,1)} %gather_fusion.2, bf16[224,128,128]{2,1,0:T(8,128)(2,1)} %param.14), kind=kOutput, calls=%fused_computation.8 | convolution fusion | flops 1879048192 | bytes 51380224 | tf_op jit(solution)/shard_map/bji,bjf->bif/dot_general | solution.py:91
  475.1 29.6 %copy.36 = f32[224,128,256]{2,1,0:T(8,128)} copy(f32[224,128,256]{1,2,0:T(8,128)} %convolution_bitcast_fusion) | data formatting | bytes 58720256 | tf_op jit(solution)/shard_map/bji,bjf->bif/dot_general | solution.py:91
  504.7 7.8 %broadcast_in_dim.34 = f32[128,128,256]{2,1,0:T(8,128)} broadcast(f32[]{:T(128)} %constant.9.clone.1), dimensions={} | broadcast | bytes 16777220 | tf_op jit(solution)/shard_map/broadcast_in_dim | solution.py:98
  512.5 67.3 %scatter_fusion.2 = f32[128,128,256]{2,1,0:T(8,128)} fusion(f32[128,128,256]{2,1,0:T(8,128)} %broadcast_in_dim.34, s32[224]{0:T(256)S(1)} %get-tuple-element.5, f32[224,128,256]{2,1,0:T(8,128)} %copy.36), kind=kCustom, calls=%fused_computation.6 | custom fusion | flops 7340032 | bytes 88081280 | tf_op jit(solution)/shard_map/scatter-add | solution.py:100
  579.9 9.6 %multiply_convert_fusion = bf16[128,128,256]{2,1,0:T(8,128)(2,1)} fusion(f32[128,128,256]{2,1,0:T(8,128)} %scatter_fusion.2), kind=kLoop, calls=%fused_computation.7 | loop fusion | flops 8388608 | bytes 25165824 | tf_op jit(solution)/shard_map/convert_element_type | solution.py:103
  589.5 5.5 all-reduce.2.cloned.1.call-done
  595.0 1.7 broadcast_multiply_fusion.1
  596.6 50.6 %reduce-scatter.2.cloned.1.call-done = bf16[16,128,256]{2,1,0:T(8,128)(2,1)} async-done(((bf16[128,128,256]{2,1,0:T(8,128)(2,1)}), bf16[16,128,256]{2,1,0:T(8,128)(2,1)}) %reduce-scatter.2.cloned.1.call-update) | async-done | bytes 1048592 | tf_op jit(solution)/shard_map/reduce_scatter | solution.py:102
  (16 shorter events, 0.1 us)
Async XLA Ops:
  11.4 97.7 %all-to-all-start = ((s32[128,1,2]{2,1,0:T(1,128)}), s32[128,1,2]{2,1,0:T(1,128)S(1)}, u32[]{:S(2)}, u32[]{:S(2)}) async-start(s32[128,1,2]{2,1,0:T(1,128)} %bitcast.3), calls=%async_computation | async-start | bytes 131072 | tf_op jit(solution)/shard_map/all_to_all | solution.py:56
  22.9 98.3 %all-gather.2.cloned.1.call-start = ((), (), s32[]{:S(2)}) async-start(), calls=%async_computation.3 | async-start | bytes 9437184 | tf_op jit(solution)/shard_map/all_gather | solution.py:29
  109.1 10.5 %copy-start.2 = (s32[224]{0:T(256)S(1)}, s32[224]{0:T(256)}, u32[]{:S(2)}) copy-start(s32[224]{0:T(256)} %param.16) | copy-start | bytes 2692
  109.1 10.5 %copy-start.3 = (s32[224]{0:T(256)S(1)}, s32[224]{0:T(256)}, u32[]{:S(2)}) copy-start(s32[224]{0:T(256)} %param.15) | copy-start | bytes 2692
  109.1 242.7 %all-to-all-start.1 = ((bf16[128,2,128,256]{3,1,2,0:T(2,128)(2,1)}), bf16[128,2,128,256]{3,1,2,0:T(2,128)(2,1)}, u32[]{:S(2)}, u32[]{:S(2)}) async-start(bf16[128,2,128,256]{3,1,2,0:T(2,128)(2,1)} %copy.30), calls=%async_computation.1 | async-start | bytes 33554432 | tf_op jit(solution)/shard_map/all_to_all | solution.py:49
  119.4 475.6 %all-reduce.2.cloned.1.call-start = ((), (), s32[]{:S(2)}) async-start(), calls=%async_computation.4 | async-start | bytes 524288 | tf_op jit(solution)/shard_map/psum | solution.py:86
  400.3 42.5 %copy-start = (bf16[2048,256]{1,0:T(8,128)(2,1)S(1)}, bf16[2048,256]{1,0:T(8,128)(2,1)}, u32[]{:S(2)}) copy-start(bf16[2048,256]{1,0:T(8,128)(2,1)} %param.12) | copy-start | bytes 3145732
  442.5 0.9 copy-start.1
  442.5 1.3 copy-start.4
  447.6 199.6 %reduce-scatter.2.cloned.1.call-start = ((), (), s32[]{:S(2)}) async-start(), calls=%async_computation.5 | async-start | bytes 9437184 | tf_op jit(solution)/shard_map/reduce_scatter | solution.py:102
Sparse Core Ops, SparseCore 0:
  25.5 51.6 all-gather.1
  447.7 147.1 all-reduce.1
  597.9 49.2 reduce-scatter.1
where the time goes:
time: 657 us; the launch traced here: 654 us
  waiting for transfers between devices  227 us (35%)
  local copies, waits for them, and re-layouts  208 us (32%)
  other arithmetic  125 us (19%)
  matrix products  57.3 us (9%)
  starting transfers between devices  22.3 us (3%)
  between operations  13.9 us (2%)
    all_to_all x1, waiting for transfers between devices, per_device(): lax.all_to_all(outgoing.reshape(devices, capacity, block_size, features),...  170 us
    scatter-add x1, other arithmetic, per_device(): term = jnp.zeros((node_blocks * lax.axis_size('mem'), block_size, feature...  67.3 us
    reduce_scatter x1, waiting for transfers between devices, per_device(): lax.psum_scatter((0.9 * term).astype(jnp.bfloat16), 'mem', scatter_dimens...  50.6 us
    scatter-add x1, other arithmetic, per_device(): jnp.zeros((node_blocks, block_size, features), jnp.float32).at[grp_row]  42.2 us
    reshape x1, local copies, waits for them, and re-layouts, per_device(): outgoing.reshape(devices, capacity, block_size, features)  30.7 us
    dot_general x1, local copies, waits for them, and re-layouts, per_device(): jnp.einsum('bji,bjf->bif', grp_vals, grad_blocks[grp_row], preferred_elem...  29.6 us
    dot_general x1, local copies, waits for them, and re-layouts, per_device(): jnp.einsum('bij,bjf->bif', grp_vals, picked, preferred_element_type=jnp.f...  29.5 us
    reshape x1, local copies, waits for them, and re-layouts, per_device(): incoming = incoming.reshape(devices * capacity, block_size, features)  24.8 us
  transfers between devices with their start and end apart: 5, of which 3 were waited for; matrix products, arithmetic and copies ran while one was open for 44% of the time, Pallas kernels for 0%

commit v1 on v0

v1 whole, which is shorter than its diff:
```python
import math

import jax
import jax.numpy as jnp
from jax import lax
from jax.experimental import pallas as pl
from jax.experimental.pallas import tpu as pltpu
from jax.sharding import PartitionSpec as P

AXES = ("grp", "mem")
VMEM_LIMIT = 56 * 1024 * 1024


def params(**kw):
    return pltpu.CompilerParams(vmem_limit_bytes=VMEM_LIMIT, **kw)


def full(shape):
    return pl.BlockSpec(shape, lambda *_: (0,) * len(shape))


def cost(flops, moved):
    return pl.CostEstimate(flops=flops, bytes_accessed=moved, transcendentals=0)


def partial_kernel(edge_ref, src_ref, vals_ref, hid_ref, out_ref):
    step = pl.program_id(0)
    per_step = out_ref.shape[0]
    blk = vals_ref.shape[1]
    for i in range(per_step):
        for k in range(2):
            edge = edge_ref[(step * per_step + i) * 2 + k]

            @pl.when(edge >= 0)
            def _():
                out_ref[i, k * blk : (k + 1) * blk, :] = jnp.dot(
                    vals_ref[edge], hid_ref[src_ref[edge]], preferred_element_type=jnp.float32
                ).astype(out_ref.dtype)


def partials(slot_edge, bnd_src, bnd_vals, blocks, devices):
    count, blk, _ = bnd_vals.shape
    nb, _, feat = blocks.shape
    per_step = 4
    return pl.pallas_call(
        partial_kernel,
        grid_spec=pltpu.PrefetchScalarGridSpec(
            num_scalar_prefetch=2,
            grid=(devices // per_step,),
            in_specs=[full(bnd_vals.shape), full(blocks.shape)],
            out_specs=pl.BlockSpec((per_step, 2 * blk, feat), lambda i, *_: (i, 0, 0)),
        ),
        out_shape=jax.ShapeDtypeStruct((devices, 2 * blk, feat), jnp.bfloat16),
        compiler_params=params(),
        cost_estimate=cost(2 * count * blk * blk * feat, devices * 4 * blk * feat),
    )(slot_edge, bnd_src, bnd_vals, blocks)


def forward_kernel(row_ref, col_ref, vals_ref, table_ref, out_ref):
    step = pl.program_id(0)
    per_step = vals_ref.shape[0]

    @pl.when(step == 0)
    def _():
        out_ref[...] = jnp.zeros_like(out_ref)

    for i in range(per_step):
        b = step * per_step + i
        row = row_ref[b]
        out_ref[row] += jnp.dot(
            vals_ref[i], table_ref[col_ref[b]], preferred_element_type=jnp.float32
        )


def group_forward(grp_row, grp_col, grp_vals, table, nb):
    count, blk, _ = grp_vals.shape
    feat = table.shape[-1]
    per_step = 16
    return pl.pallas_call(
        forward_kernel,
        grid_spec=pltpu.PrefetchScalarGridSpec(
            num_scalar_prefetch=2,
            grid=(count // per_step,),
            in_specs=[
                pl.BlockSpec((per_step, blk, blk), lambda i, *_: (i, 0, 0)),
                full(table.shape),
            ],
            out_specs=full((nb, blk, feat)),
        ),
        out_shape=jax.ShapeDtypeStruct((nb, blk, feat), jnp.float32),
        compiler_params=params(),
        cost_estimate=cost(2 * count * blk * blk * feat, 40_000_000),
    )(grp_row, grp_col, grp_vals, table)


def mid_kernel(
    total_nodes,
    rows_ref,
    inc_ref,
    summed_ref,
    initial_ref,
    cot_ref,
    w_ref,
    out_ref,
    gmix_ref,
    gw_ref,
    acc,
    mw,
):
    step = pl.program_id(0)
    per_step = inc_ref.shape[0]
    nb, blk, feat = acc.shape

    @pl.when(step == 0)
    def _():
        acc[...] = summed_ref[...]

    for i in range(per_step):
        for k in range(2):
            row = rows_ref[(step * per_step + i) * 2 + k]

            @pl.when(row >= 0)
            def _():
                acc[row] += inc_ref[i, k * blk : (k + 1) * blk, :].astype(jnp.float32)

    @pl.when(step == pl.num_programs(0) - 1)
    def _():
        eye = lax.broadcasted_iota(jnp.int32, (feat, feat), 0) == lax.broadcasted_iota(
            jnp.int32, (feat, feat), 1
        )
        mw[...] = (
            jnp.where(eye, 0.5, 0.0).astype(jnp.float32) + 0.5 * w_ref[...].astype(jnp.float32)
        ).astype(jnp.bfloat16)
        gw_ref[...] = jnp.zeros_like(gw_ref)

        def body(j, _):
            at = pl.ds(pl.multiple_of(j * blk, blk), blk)
            mixed = (0.9 * acc[j] + 0.1 * initial_ref[at, :].astype(jnp.float32)).astype(
                jnp.bfloat16
            )
            pre = jnp.dot(mixed, mw[...], preferred_element_type=jnp.float32)
            sig = jax.nn.sigmoid(pre)
            out_ref[at, :] = (pre * sig).astype(jnp.bfloat16)
            gpre = (cot_ref[at, :].astype(jnp.float32) * sig * (1.0 + pre * (1.0 - sig))).astype(
                jnp.bfloat16
            )
            gw_ref[...] += lax.dot_general(
                mixed, gpre, (((0,), (0,)), ((), ())), preferred_element_type=jnp.float32
            )
            gmix_ref[at, :] = lax.dot_general(
                gpre, mw[...], (((1,), (1,)), ((), ())), preferred_element_type=jnp.float32
            ).astype(jnp.bfloat16)
            return 0

        lax.fori_loop(0, nb, body, 0)


def middle(in_rows, incoming, summed, initial, cotangent, weight, total_nodes):
    devices, two_blk, feat = incoming.shape
    nb, blk, _ = summed.shape
    nodes = nb * blk
    per_step = 8
    return pl.pallas_call(
        lambda *refs: mid_kernel(total_nodes, *refs),
        grid_spec=pltpu.PrefetchScalarGridSpec(
            num_scalar_prefetch=1,
            grid=(devices // per_step,),
            in_specs=[
                pl.BlockSpec((per_step, two_blk, feat), lambda i, *_: (i, 0, 0)),
                full(summed.shape),
                full(initial.shape),
                full(cotangent.shape),
                full(weight.shape),
            ],
            out_specs=[full((nodes, feat)), full((nodes, feat)), full((feat, feat))],
            scratch_shapes=[
                pltpu.VMEM((nb, blk, feat), jnp.float32),
                pltpu.VMEM((feat, feat), jnp.bfloat16),
            ],
        ),
        out_shape=[
            jax.ShapeDtypeStruct((nodes, feat), jnp.bfloat16),
            jax.ShapeDtypeStruct((nodes, feat), jnp.bfloat16),
            jax.ShapeDtypeStruct((feat, feat), jnp.float32),
        ],
        compiler_params=params(),
        cost_estimate=cost(6 * nodes * feat * feat, 30_000_000),
    )(in_rows, incoming, summed, initial, cotangent, weight)


def backward_kernel(row_ref, col_ref, vals_ref, gmix_ref, out_ref, acc):
    step = pl.program_id(0)
    per_step = vals_ref.shape[0]

    @pl.when(step == 0)
    def _():
        def zero(j, _):
            acc[j] = jnp.zeros(acc.shape[1:], acc.dtype)
            return 0

        lax.fori_loop(0, acc.shape[0], zero, 0)

    for i in range(per_step):
        b = step * per_step + i
        col = col_ref[b]
        acc[col] += lax.dot_general(
            vals_ref[i],
            gmix_ref[row_ref[b]],
            (((0,), (0,)), ((), ())),
            preferred_element_type=jnp.float32,
        )

    @pl.when(step == pl.num_programs(0) - 1)
    def _():
        def write(j, _):
            out_ref[j] = (0.9 * acc[j]).astype(out_ref.dtype)
            return 0

        lax.fori_loop(0, acc.shape[0], write, 0)


def group_backward(grp_row, grp_col, grp_vals, gmix, members):
    count, blk, _ = grp_vals.shape
    nb, _, feat = gmix.shape
    per_step = 16
    return pl.pallas_call(
        backward_kernel,
        grid_spec=pltpu.PrefetchScalarGridSpec(
            num_scalar_prefetch=2,
            grid=(count // per_step,),
            in_specs=[
                pl.BlockSpec((per_step, blk, blk), lambda i, *_: (i, 0, 0)),
                full(gmix.shape),
            ],
            out_specs=full((nb * members, blk, feat)),
            scratch_shapes=[pltpu.VMEM((nb * members, blk, feat), jnp.float32)],
        ),
        out_shape=jax.ShapeDtypeStruct((nb * members, blk, feat), jnp.bfloat16),
        compiler_params=params(),
        cost_estimate=cost(2 * count * blk * blk * feat, 40_000_000),
    )(grp_row, grp_col, grp_vals, gmix)


def first_and_last(mask, key, axis):
    big = jnp.int32(1 << 30)
    low = jnp.min(jnp.where(mask, key, big), axis=axis)
    high = jnp.max(jnp.where(mask, key, -1), axis=axis)
    return jnp.where(low == big, -1, low), jnp.where(high == low, -1, high)


def per_device(
    hidden,
    initial,
    weight,
    grp_vals,
    grp_row,
    grp_col,
    bnd_vals,
    bnd_src,
    bnd_dst,
    bnd_row,
    cotangent,
):
    blk = grp_vals.shape[1]
    nodes, feat = hidden.shape
    nb = nodes // blk
    devices = lax.axis_size(AXES)
    members = lax.axis_size("mem")
    count = bnd_vals.shape[0]
    me = lax.axis_index(AXES)
    blocks = hidden.reshape(nb, blk, feat)

    target = bnd_dst[:, 0]
    ids = jnp.arange(count, dtype=jnp.int32)
    slot_edge = jnp.stack(
        first_and_last(
            target[None, :] == jnp.arange(devices, dtype=jnp.int32)[:, None],
            jnp.broadcast_to(ids[None, :], (devices, count)),
            1,
        ),
        axis=1,
    ).reshape(-1)
    table = lax.all_gather(blocks, "mem", axis=0, tiled=True)
    codes = lax.all_gather(target * nb + bnd_row, AXES, axis=0, tiled=False)

    outgoing = partials(slot_edge, bnd_src, bnd_vals, blocks, devices)
    incoming = lax.all_to_all(outgoing, AXES, split_axis=0, concat_axis=0, tiled=True)
    summed = group_forward(grp_row, grp_col, grp_vals, table, nb)

    low, high = first_and_last(codes // nb == me, ids[None, :] * nb + codes % nb, 1)
    in_rows = jnp.stack(
        [jnp.where(low < 0, -1, low % nb), jnp.where(high < 0, -1, high % nb)], axis=1
    ).reshape(-1)

    output, gmix, local_weight = middle(
        in_rows, incoming, summed, initial, cotangent, weight, nodes * devices
    )
    grad_weight = 0.5 * lax.psum(local_weight, AXES) / math.sqrt(nodes * devices)
    term = group_backward(grp_row, grp_col, grp_vals, gmix.reshape(nb, blk, feat), members)
    grad_table = lax.psum_scatter(term, "mem", scatter_dimension=0, tiled=True)
    return output, grad_weight, grad_table.reshape(nodes, feat)


def solution(mesh):
    return jax.shard_map(
        per_device,
        mesh=mesh,
        in_specs=(
            P(AXES, None),
            P(AXES, None),
            P(),
            P(AXES, None, None),
            P(AXES),
            P(AXES),
            P(AXES, None, None),
            P(AXES),
            P(AXES, None),
            P(AXES),
            P(AXES, None),
        ),
        out_specs=(P(AXES, None), P(), P(AXES, None)),
        check_vma=False,
    )
```

time: 657 us -> 583 us (0.89)
  blocking collectives: 0 us -> 296 us
  local copies, waits for them, and re-layouts: 208 us -> 1.75 us
  other arithmetic: 125 us -> 2.76 us
  Pallas kernels: 0 us -> 83.4 us
  matrix products: 57.3 us -> 0 us
  waiting for transfers between devices: 227 us -> 171 us
  starting transfers between devices: 22.3 us -> 12.6 us
    unnamed x0 -> x1, blocking collectives: none -> 296 us
    all_to_all x2 -> x1, waiting for transfers between devices: 170 us -> 0.01 us  [per_device(): lax.all_to_all(outgoing, AXES, split_axis=0, concat_axis=0, tiled=True)]
    psum x1, waiting for transfers between devices: 5.47 us -> 120 us  [per_device(): lax.psum(local_weight, AXES)]
    scatter-add x2 -> x0, other arithmetic: 109 us -> none  [the longest x1 67.3 us: per_device(): term = jnp.zeros((node_blocks * lax.axis_size('mem'), block_size, feature...]
    pallas_call x0 -> x4, Pallas kernels: none -> 83.4 us  [the longest x1 26.1 us: partials(): pl.pallas_call(partial_kernel, grid_spec=pltpu.PrefetchScalarGridSpec(num...]
    dot_general x3 -> x0, local copies, waits for them, and re-layouts: 60.3 us -> none  [the longest x1 29.6 us: per_device(): jnp.einsum('bji,bjf->bif', grp_vals, grad_blocks[grp_row], preferred_elem...]
    dot_general x7 -> x0, matrix products: 57.3 us -> none  [the longest x1 18.1 us: per_device(): jnp.einsum('bji,bjf->bif', grp_vals, grad_blocks[grp_row], preferred_elem...]
    reshape x2, local copies, waits for them, and re-layouts: 55.5 us -> 1.43 us  [the longest x1 0.72 us: per_device(): in_rows = jnp.stack([jnp.where(low < 0, -1, low % nb), jnp.where(high < 0...]
  transfers between devices with their start and end apart: 5 -> 4, of which waited for: 3 -> 2; matrix products, arithmetic and copies ran while one was open for 44% -> 0% of each run, Pallas kernels for 0% -> 6%
where the time goes in v1:
time: 583 us; the launch traced here: 582 us
  blocking collectives  296 us (51%)
  waiting for transfers between devices  171 us (29%)
  Pallas kernels  83.4 us (14%)
  between operations  13.8 us (2%)
  starting transfers between devices  12.6 us (2%)
    unnamed x1, blocking collectives  296 us
    psum x1, waiting for transfers between devices, per_device(): lax.psum(local_weight, AXES)  120 us
    reduce_scatter x1, waiting for transfers between devices, per_device(): grad_table = lax.psum_scatter(term, 'mem', scatter_dimension=0, tiled=True)  50.6 us
    pallas_call x1, Pallas kernels, partials(): pl.pallas_call(partial_kernel, grid_spec=pltpu.PrefetchScalarGridSpec(num...  26.1 us
    pallas_call x1, Pallas kernels, middle(): pl.pallas_call(lambda *refs: mid_kernel(total_nodes, *refs), grid_spec=pl...  22.6 us
    pallas_call x1, Pallas kernels, group_backward(): pl.pallas_call(backward_kernel, grid_spec=pltpu.PrefetchScalarGridSpec(nu...  18.9 us
    pallas_call x1, Pallas kernels, group_forward(): pl.pallas_call(forward_kernel, grid_spec=pltpu.PrefetchScalarGridSpec(num...  15.8 us
    all_to_all x1, starting transfers between devices, per_device(): lax.all_to_all(outgoing, AXES, split_axis=0, concat_axis=0, tiled=True)  12.4 us
  transfers between devices with their start and end apart: 4, of which 2 were waited for; matrix products, arithmetic and copies ran while one was open for 0% of the time, Pallas kernels for 6%

profile of v1, /device:TPU:1, one launch (start us, length us, event | category | flops | bytes accessed | tf_op | source)
XLA Modules:
  0.0 582.2 jit_solution(6089596623491806427)
XLA Ops:
  7.2 0.8 select_reduce_fusion.1
  8.0 0.1 copy.17
  8.1 0.7 reshape.150.edge_ref
  8.8 26.1 %shard_map.130 = bf16[128,256,256]{2,1,0:T(8,128)(2,1)} custom-call(s32[256]{0:T(256)} %reshape.150.edge_ref, s32[112]{0:T(128)} %src_ref.1, bf16[112,128,128]{2,1,0:T(8,128)(2,1)} %vals_ref.3, bf16[16,128,256]{2,1,0:T(8,128)(2,1)} %bitcast.15), custom_call_target="tpu_custom_call" | custom-call | flops 939524096 | bytes 16777216 | tf_op jit(solution)/shard_map/pallas_call | solution.py:45
  34.9 0.0 copy-start
  34.9 0.0 copy-start.1
  34.9 12.4 %all-to-all-start = ((bf16[128,256,256]{2,1,0:T(8,128)(2,1)}), bf16[128,256,256]{2,1,0:T(8,128)(2,1)}, u32[]{:S(2)}, u32[]{:S(2)}) async-start(bf16[128,256,256]{2,1,0:T(8,128)(2,1)} %shard_map.130), calls=%async_computation | async-start | bytes 33554432 | tf_op jit(solution)/shard_map/all_to_all | solution.py:287
  47.3 0.0 all-gather.3.cloned.1.call-start
  47.4 0.7 all-gather.3.cloned.1.call-update
  48.1 0.0 all-reduce.3.cloned.1.call-start
  48.1 0.0 copy-done
  48.1 0.0 copy-done.1
  48.2 0.1 add_dynamic-update-slice_fusion
  48.3 296.5 %all-reduce = s32[14336]{0:T(1024)S(1)} all-reduce(s32[14336]{0:T(1024)S(1)} %add_dynamic-update-slice_fusion), channel_id=2, replica_groups=mesh['grp'=16,'mem'=8] {'grp','mem'}, use_global_device_ids=true, to_apply=%add | all-reduce | flops 14336 | bytes 114688
  344.8 0.1 reshape.154
  344.9 0.2 select_reduce_fusion.3
  345.1 0.1 copy.16
  345.2 0.7 reshape.149.refs_0_
  345.9 0.0 all-gather.3.cloned.1.call-done.table_ref
  345.9 15.8 %shard_map.131.refs_2_ = f32[16,128,256]{2,1,0:T(8,128)} custom-call(s32[224]{0:T(256)} %row_ref.3, s32[224]{0:T(256)} %col_ref.3, bf16[224,128,128]{2,1,0:T(8,128)(2,1)} %vals_ref.5, bf16[128,128,256]{2,1,0:T(8,128)(2,1)} %all-gather.3.cloned.1.call-done.table_ref), custom_call_target="tpu_custom_call" | custom-call | flops 1879048192 | bytes 40000000 | tf_op jit(solution)/shard_map/pallas_call | solution.py:79
  361.7 0.0 all-to-all-done.refs_1_
  361.7 22.6 %shard_map.132 = (bf16[2048,256]{1,0:T(8,128)(2,1)}, bf16[2048,256]{1,0:T(8,128)(2,1)}, f32[256,256]{1,0:T(8,128)}) custom-call(s32[256]{0:T(256)} %reshape.149.refs_0_, bf16[128,256,256]{2,1,0:T(8,128)(2,1)} %all-to-all-done.refs_1_, f32[16,128,256]{2,1,0:T(8,128)} %shard_map.131.refs_2_, bf16[2048,256]{1,0:T(8,128)(2,1)} %refs_3_.1, ...), custom_call_target="tpu_custom_call" | custom-call | flops 805306368 | bytes 30000000 | tf_op jit(solution)/shard_map/pallas_call | solution.py:163
  384.3 0.0 all-reduce.3.cloned.1.call-update
  384.3 0.0 reduce-scatter.2.cloned.1.call-start
  384.4 18.9 %shard_map.133 = bf16[128,128,256]{2,1,0:T(8,128)(2,1)} custom-call(s32[224]{0:T(256)} %row_ref.3, s32[224]{0:T(256)} %col_ref.3, bf16[224,128,128]{2,1,0:T(8,128)(2,1)} %vals_ref.5, bf16[16,128,256]{2,1,0:T(8,128)(2,1)} %bitcast.17), custom_call_target="tpu_custom_call" | custom-call | flops 1879048192 | bytes 40000000 | tf_op jit(solution)/shard_map/pallas_call | solution.py:226
  403.2 0.0 reduce-scatter.2.cloned.1.call-update
  403.3 120.1 %all-reduce.3.cloned.1.call-done = f32[256,256]{1,0:T(8,128)} async-done(((f32[256,256]{1,0:T(8,128)}), f32[256,256]{1,0:T(8,128)}) %all-reduce.3.cloned.1.call-update) | async-done | bytes 262160 | tf_op jit(solution)/shard_map/psum | solution.py:298
  523.4 1.7 broadcast_multiply_fusion
  525.0 50.6 %reduce-scatter.2.cloned.1.call-done = bf16[16,128,256]{2,1,0:T(8,128)(2,1)} async-done(((bf16[128,128,256]{2,1,0:T(8,128)(2,1)}), bf16[16,128,256]{2,1,0:T(8,128)(2,1)}) %reduce-scatter.2.cloned.1.call-update) | async-done | bytes 1048592 | tf_op jit(solution)/shard_map/reduce_scatter | solution.py:300
  (6 shorter events, 0.0 us)
Async XLA Ops:
  34.9 13.3 %copy-start = (s32[112]{0:T(128)S(1)}, s32[112]{0:T(128)}, u32[]{:S(2)}) copy-start(s32[112]{0:T(128)} %param.20) | copy-start | bytes 1348
  34.9 13.3 %copy-start.1 = (s32[112,1]{0,1:T(1,128)S(1)}, s32[112,1]{0,1:T(1,128)}, u32[]{:S(2)}) copy-start(s32[112,1]{0,1:T(1,128)} %param.19) | copy-start | bytes 1348
  34.9 326.8 %all-to-all-start = ((bf16[128,256,256]{2,1,0:T(8,128)(2,1)}), bf16[128,256,256]{2,1,0:T(8,128)(2,1)}, u32[]{:S(2)}, u32[]{:S(2)}) async-start(bf16[128,256,256]{2,1,0:T(8,128)(2,1)} %shard_map.130), calls=%async_computation | async-start | bytes 33554432 | tf_op jit(solution)/shard_map/all_to_all | solution.py:287
  47.3 298.6 %all-gather.3.cloned.1.call-start = ((), (), s32[]{:S(2)}) async-start(), calls=%async_computation.2 | async-start | bytes 9437184 | tf_op jit(solution)/shard_map/all_gather | solution.py:283
  48.1 475.3 %all-reduce.3.cloned.1.call-start = ((), (), s32[]{:S(2)}) async-start(), calls=%async_computation.3 | async-start | bytes 524288 | tf_op jit(solution)/shard_map/psum | solution.py:298
  384.3 191.3 %reduce-scatter.2.cloned.1.call-start = ((), (), s32[]{:S(2)}) async-start(), calls=%async_computation.4 | async-start | bytes 9437184 | tf_op jit(solution)/shard_map/reduce_scatter | solution.py:300
Sparse Core Ops, SparseCore 0:
  49.9 219.6 all-gather.2
  384.5 138.8 all-reduce.2
  526.3 49.2 reduce-scatter.1

commit v2 on v1

--- a/solution.py
+++ b/solution.py
@@ -8,6 +8,7 @@
 from jax.sharding import PartitionSpec as P
 
 AXES = ("grp", "mem")
+MESH = pl.DeviceIdType.MESH
 VMEM_LIMIT = 56 * 1024 * 1024
 
 
@@ -23,37 +24,60 @@
     return pl.CostEstimate(flops=flops, bytes_accessed=moved, transcendentals=0)
 
 
-def partial_kernel(edge_ref, src_ref, vals_ref, hid_ref, out_ref):
+def partial_kernel(slot_ref, src_ref, vals_ref, hid_ref, out_ref, stage, sem):
     step = pl.program_id(0)
-    per_step = out_ref.shape[0]
-    blk = vals_ref.shape[1]
+    half = lax.rem(step, 2)
+    per_step = vals_ref.shape[0]
+
+    def drain(which):
+        for i in range(per_step):
+            pltpu.make_async_copy(stage.at[which, i], out_ref.at[0], sem.at[which, i]).wait()
+
+    @pl.when(step >= 2)
+    def _():
+        drain(half)
+
     for i in range(per_step):
-        for k in range(2):
-            edge = edge_ref[(step * per_step + i) * 2 + k]
-
-            @pl.when(edge >= 0)
-            def _():
-                out_ref[i, k * blk : (k + 1) * blk, :] = jnp.dot(
-                    vals_ref[edge], hid_ref[src_ref[edge]], preferred_element_type=jnp.float32
-                ).astype(out_ref.dtype)
-
-
-def partials(slot_edge, bnd_src, bnd_vals, blocks, devices):
+        edge = step * per_step + i
+        stage[half, i] = jnp.dot(
+            vals_ref[i], hid_ref[src_ref[edge]], preferred_element_type=jnp.float32
+        ).astype(stage.dtype)
+    for i in range(per_step):
+        edge = step * per_step + i
+        pltpu.make_async_copy(
+            stage.at[half, i], out_ref.at[slot_ref[edge]], sem.at[half, i]
+        ).start()
+
+    @pl.when(step == pl.num_programs(0) - 1)
+    def _():
+        drain(1 - half)
+        drain(half)
+
+
+def partials(slot, bnd_src, bnd_vals, blocks, devices):
     count, blk, _ = bnd_vals.shape
     nb, _, feat = blocks.shape
-    per_step = 4
+    per_step = 8
+    assert count % per_step == 0 and count >= 2 * per_step
     return pl.pallas_call(
         partial_kernel,
         grid_spec=pltpu.PrefetchScalarGridSpec(
             num_scalar_prefetch=2,
-            grid=(devices // per_step,),
-            in_specs=[full(bnd_vals.shape), full(blocks.shape)],
-            out_specs=pl.BlockSpec((per_step, 2 * blk, feat), lambda i, *_: (i, 0, 0)),
-        ),
-        out_shape=jax.ShapeDtypeStruct((devices, 2 * blk, feat), jnp.bfloat16),
+            grid=(count // per_step,),
+            in_specs=[
+                pl.BlockSpec((per_step, blk, blk), lambda i, *_: (i, 0, 0)),
+                full(blocks.shape),
+            ],
+            out_specs=pl.BlockSpec(memory_space=pl.ANY),
+            scratch_shapes=[
+                pltpu.VMEM((2, per_step, blk, feat), jnp.bfloat16),
+                pltpu.SemaphoreType.DMA((2, per_step)),
+            ],
+        ),
+        out_shape=jax.ShapeDtypeStruct((devices * 2, blk, feat), jnp.bfloat16),
         compiler_params=params(),
-        cost_estimate=cost(2 * count * blk * blk * feat, devices * 4 * blk * feat),
-    )(slot_edge, bnd_src, bnd_vals, blocks)
+        cost_estimate=cost(2 * count * blk * blk * feat, 3 * count * blk * feat),
+    )(slot, bnd_src, bnd_vals, blocks)
 
 
 def forward_kernel(row_ref, col_ref, vals_ref, table_ref, out_ref):
@@ -133,9 +157,12 @@
         ).astype(jnp.bfloat16)
         gw_ref[...] = jnp.zeros_like(gw_ref)
 
+        tall = 2 * blk
+
         def body(j, _):
-            at = pl.ds(pl.multiple_of(j * blk, blk), blk)
-            mixed = (0.9 * acc[j] + 0.1 * initial_ref[at, :].astype(jnp.float32)).astype(
+            at = pl.ds(pl.multiple_of(j * tall, tall), tall)
+            summed = acc[pl.ds(2 * j, 2)].reshape(tall, feat)
+            mixed = (0.9 * summed + 0.1 * initial_ref[at, :].astype(jnp.float32)).astype(
                 jnp.bfloat16
             )
             pre = jnp.dot(mixed, mw[...], preferred_element_type=jnp.float32)
@@ -152,7 +179,7 @@
             ).astype(jnp.bfloat16)
             return 0
 
-        lax.fori_loop(0, nb, body, 0)
+        lax.fori_loop(0, nb // 2, body, 0)
 
 
 def middle(in_rows, incoming, summed, initial, cotangent, weight, total_nodes):
@@ -188,7 +215,7 @@
     )(in_rows, incoming, summed, initial, cotangent, weight)
 
 
-def backward_kernel(row_ref, col_ref, vals_ref, gmix_ref, out_ref, acc):
+def backward_kernel(part, nb, size, row_ref, col_ref, vals_ref, gmix_ref, out_ref, acc):
     step = pl.program_id(0)
     per_step = vals_ref.shape[0]
 
@@ -203,12 +230,16 @@
     for i in range(per_step):
         b = step * per_step + i
         col = col_ref[b]
-        acc[col] += lax.dot_general(
-            vals_ref[i],
-            gmix_ref[row_ref[b]],
-            (((0,), (0,)), ((), ())),
-            preferred_element_type=jnp.float32,
-        )
+        owner, inner = col // nb, lax.rem(col, nb)
+
+        @pl.when(inner // size == part)
+        def _():
+            acc[owner * size + inner - part * size] += lax.dot_general(
+                vals_ref[i],
+                gmix_ref[row_ref[b]],
+                (((0,), (0,)), ((), ())),
+                preferred_element_type=jnp.float32,
+            )
 
     @pl.when(step == pl.num_programs(0) - 1)
     def _():
@@ -219,12 +250,14 @@
         lax.fori_loop(0, acc.shape[0], write, 0)
 
 
-def group_backward(grp_row, grp_col, grp_vals, gmix, members):
+def group_backward(part, parts, grp_row, grp_col, grp_vals, gmix, members):
     count, blk, _ = grp_vals.shape
     nb, _, feat = gmix.shape
     per_step = 16
+    size = nb // parts
+    shape = (members * size, blk, feat)
     return pl.pallas_call(
-        backward_kernel,
+        lambda *refs: backward_kernel(part, nb, size, *refs),
         grid_spec=pltpu.PrefetchScalarGridSpec(
             num_scalar_prefetch=2,
             grid=(count // per_step,),
@@ -232,20 +265,105 @@
                 pl.BlockSpec((per_step, blk, blk), lambda i, *_: (i, 0, 0)),
                 full(gmix.shape),
             ],
-            out_specs=full((nb * members, blk, feat)),
-            scratch_shapes=[pltpu.VMEM((nb * members, blk, feat), jnp.float32)],
-        ),
-        out_shape=jax.ShapeDtypeStruct((nb * members, blk, feat), jnp.bfloat16),
+            out_specs=full(shape),
+            scratch_shapes=[pltpu.VMEM(shape, jnp.float32)],
+        ),
+        out_shape=jax.ShapeDtypeStruct(shape, jnp.bfloat16),
         compiler_params=params(),
-        cost_estimate=cost(2 * count * blk * blk * feat, 40_000_000),
+        cost_estimate=cost(2 * count * blk * blk * feat // parts, 40_000_000 // parts),
     )(grp_row, grp_col, grp_vals, gmix)
 
 
-def first_and_last(mask, key, axis):
-    big = jnp.int32(1 << 30)
-    low = jnp.min(jnp.where(mask, key, big), axis=axis)
-    high = jnp.max(jnp.where(mask, key, -1), axis=axis)
-    return jnp.where(low == big, -1, low), jnp.where(high == low, -1, high)
+def reduce_kernel(groups, members, scale, x_ref, out_ref, part, whole, done, sems):
+    g, m = lax.axis_index("grp"), lax.axis_index("mem")
+    rows = part.shape[1]
+    barrier = pltpu.get_barrier_semaphore()
+    mates = [lax.rem(m + k, members) for k in range(1, members)]
+    peers = [lax.rem(g + k, groups) for k in range(1, groups)]
+    for mate in mates:
+        pl.semaphore_signal(barrier, inc=1, device_id=(g, mate), device_id_type=MESH)
+    for peer in peers:
+        pl.semaphore_signal(barrier, inc=1, device_id=(peer, m), device_id_type=MESH)
+    pl.semaphore_wait(barrier, members + groups - 2)
+
+    def at(index):
+        return pl.ds(pl.multiple_of(index * rows, rows), rows)
+
+    copies = []
+    for k, mate in enumerate(mates):
+        copies.append(
+            pltpu.make_async_remote_copy(
+                x_ref.at[at(mate)],
+                part.at[m],
+                sems.at[0, k],
+                sems.at[1, k],
+                device_id=(g, mate),
+                device_id_type=MESH,
+            )
+        )
+        copies[-1].start()
+    part[m] = x_ref[at(m), :]
+    for copy in copies:
+        copy.wait()
+    total = part[0]
+    for k in range(1, members):
+        total = total + part[k]
+    whole[g] = total
+    copies = []
+    for k, peer in enumerate(peers):
+        copies.append(
+            pltpu.make_async_remote_copy(
+                whole.at[g],
+                whole.at[g],
+                sems.at[2, k],
+                sems.at[3, k],
+                device_id=(peer, m),
+                device_id_type=MESH,
+            )
+        )
+        copies[-1].start()
+    for copy in copies:
+        copy.wait()
+    total = whole[0]
+    for k in range(1, groups):
+        total = total + whole[k]
+    done[m] = total * scale
+    copies = []
+    for k, mate in enumerate(mates):
+        copies.append(
+            pltpu.make_async_remote_copy(
+                done.at[m],
+                done.at[m],
+                sems.at[4, k],
+                sems.at[5, k],
+                device_id=(g, mate),
+                device_id_type=MESH,
+            )
+        )
+        copies[-1].start()
+    for copy in copies:
+        copy.wait()
+    for k in range(members):
+        out_ref[k * rows : (k + 1) * rows, :] = done[k]
+
+
+def all_reduce(x, scale, groups, members):
+    rows, cols = x.shape
+    share = rows // members
+    return pl.pallas_call(
+        lambda *refs: reduce_kernel(groups, members, scale, *refs),
+        out_shape=jax.ShapeDtypeStruct(x.shape, x.dtype),
+        in_specs=[pl.BlockSpec(memory_space=pltpu.VMEM)],
+        out_specs=pl.BlockSpec(memory_space=pltpu.VMEM),
+        scratch_shapes=[
+            pltpu.VMEM((members, share, cols), jnp.float32),
+            pltpu.VMEM((groups, share, cols), jnp.float32),
+            pltpu.VMEM((members, share, cols), jnp.float32),
+            pltpu.SemaphoreType.DMA((6, max(groups, members) - 1)),
+        ],
+        compiler_params=params(collective_id=0, has_side_effects=True),
+        cost_estimate=cost(1_000_000, 4_000_000),
+    )(x)
 
 
 def per_device(
@@ -265,40 +383,48 @@
     nodes, feat = hidden.shape
     nb = nodes // blk
     devices = lax.axis_size(AXES)
-    members = lax.axis_size("mem")
+    groups, members = lax.axis_size("grp"), lax.axis_size("mem")
     count = bnd_vals.shape[0]
-    me = lax.axis_index(AXES)
     blocks = hidden.reshape(nb, blk, feat)
 
     target = bnd_dst[:, 0]
     ids = jnp.arange(count, dtype=jnp.int32)
-    slot_edge = jnp.stack(
-        first_and_last(
-            target[None, :] == jnp.arange(devices, dtype=jnp.int32)[:, None],
-            jnp.broadcast_to(ids[None, :], (devices, count)),
-            1,
-        ),
+    place = jnp.sum(
+        (target[:, None] == target[None, :]) & (ids[None, :] < ids[:, None]),
         axis=1,
+        dtype=jnp.int32,
+    )
+    slot = target * 2 + place
+    out_rows = jnp.max(
+        jnp.where(
+            slot[None, :] == jnp.arange(2 * devices, dtype=jnp.int32)[:, None],
+            bnd_row[None, :],
+            -1,
+        ),
+        axis=1,
+    )
+    in_rows = lax.all_to_all(
+        out_rows.reshape(devices, 2), AXES, split_axis=0, concat_axis=0, tiled=True
     ).reshape(-1)
     table = lax.all_gather(blocks, "mem", axis=0, tiled=True)
-    codes = lax.all_gather(target * nb + bnd_row, AXES, axis=0, tiled=False)
-
-    outgoing = partials(slot_edge, bnd_src, bnd_vals, blocks, devices)
-    incoming = lax.all_to_all(outgoing, AXES, split_axis=0, concat_axis=0, tiled=True)
+    outgoing = partials(slot, bnd_src, bnd_vals, blocks, devices)
+    outgoing, table, in_rows = lax.optimization_barrier((outgoing, table, in_rows))
+    incoming = lax.all_to_all(
+        outgoing.reshape(devices, 2 * blk, feat), AXES, split_axis=0, concat_axis=0, tiled=True
+    )
     summed = group_forward(grp_row, grp_col, grp_vals, table, nb)
-
-    low, high = first_and_last(codes // nb == me, ids[None, :] * nb + codes % nb, 1)
-    in_rows = jnp.stack(
-        [jnp.where(low < 0, -1, low % nb), jnp.where(high < 0, -1, high % nb)], axis=1
-    ).reshape(-1)
-
     output, gmix, local_weight = middle(
         in_rows, incoming, summed, initial, cotangent, weight, nodes * devices
     )
-    grad_weight = 0.5 * lax.psum(local_weight, AXES) / math.sqrt(nodes * devices)
-    term = group_backward(grp_row, grp_col, grp_vals, gmix.reshape(nb, blk, feat), members)
-    grad_table = lax.psum_scatter(term, "mem", scatter_dimension=0, tiled=True)
-    return output, grad_weight, grad_table.reshape(nodes, feat)
+    gmix = gmix.reshape(nb, blk, feat)
+    parts = 2
+    tables = []
+    for part in range(parts):
+        term = group_backward(part, parts, grp_row, grp_col, grp_vals, gmix, members)
+        tables.append(lax.psum_scatter(term, "mem", scatter_dimension=0, tiled=True))
+    local_weight, term = lax.optimization_barrier((local_weight, term))
+    grad_weight = all_reduce(local_weight, 0.5 / math.sqrt(nodes * devices), groups, members)
+    return output, grad_weight, jnp.concatenate(tables, axis=0).reshape(nodes, feat)
 
 
 def solution(mesh):

time: 583 us -> 452 us (0.78)
  blocking collectives: 296 us -> 0 us
  waiting for transfers between devices: 171 us -> 266 us
  Pallas kernels: 83.4 us -> 140 us
  starting transfers between devices: 12.6 us -> 19.7 us
    unnamed x1 -> x0, blocking collectives: 296 us -> none
    all_to_all x1 -> x2, waiting for transfers between devices: 0.01 us -> 217 us  [the longest x1 217 us: per_device(): lax.all_to_all(outgoing.reshape(devices, 2 * blk, feat), AXES, split_axis...]
    psum x1 -> x0, waiting for transfers between devices: 120 us -> none  [per_device(): lax.psum(local_weight, AXES)]
    pallas_call x1 -> x3, Pallas kernels: 18.9 us -> 92.3 us  [the longest x2 61.3 us: group_backward(): pl.pallas_call(lambda *refs: backward_kernel(part, nb, size, *refs), grid...]
    reduce_scatter x1 -> x2, waiting for transfers between devices: 50.6 us -> 22.4 us  [per_device(): lax.psum_scatter(term, 'mem', scatter_dimension=0, tiled=True)]
    all_gather x1, waiting for transfers between devices: 0.01 us -> 26.4 us  [per_device(): table = lax.all_gather(blocks, 'mem', axis=0, tiled=True)]
    pallas_call x1, Pallas kernels: 26.1 us -> 12.6 us  [partials(): pl.pallas_call(partial_kernel, grid_spec=pltpu.PrefetchScalarGridSpec(num...]
    all_to_all x1 -> x2, starting transfers between devices: 12.4 us -> 19.5 us  [the longest x1 11.5 us: per_device(): lax.all_to_all(out_rows.reshape(devices, 2), AXES, split_axis=0, concat_a...]
  transfers between devices with their start and end apart: 4 -> 5, of which waited for: 2 -> 3; matrix products, arithmetic and copies ran while one was open for 0% -> 1% of each run, Pallas kernels for 6% -> 20%
where the time goes in v2:
time: 452 us; the launch traced here: 449 us
  waiting for transfers between devices  266 us (59%)
  Pallas kernels  140 us (31%)
  starting transfers between devices  19.7 us (4%)
  between operations  13.8 us (3%)
  other arithmetic  5.41 us (1%)
    all_to_all x1, waiting for transfers between devices, per_device(): lax.all_to_all(outgoing.reshape(devices, 2 * blk, feat), AXES, split_axis...  217 us
    pallas_call x2, Pallas kernels, group_backward(): pl.pallas_call(lambda *refs: backward_kernel(part, nb, size, *refs), grid...  61.3 us
    pallas_call x1, Pallas kernels, all_reduce(): pl.pallas_call(lambda *refs: reduce_kernel(groups, members, scale, *refs)...  31 us
    all_gather x1, waiting for transfers between devices, per_device(): table = lax.all_gather(blocks, 'mem', axis=0, tiled=True)  26.4 us
    reduce_scatter x2, waiting for transfers between devices, per_device(): lax.psum_scatter(term, 'mem', scatter_dimension=0, tiled=True)  22.4 us
    pallas_call x1, Pallas kernels, middle(): pl.pallas_call(lambda *refs: mid_kernel(total_nodes, *refs), grid_spec=pl...  19.7 us
    pallas_call x1, Pallas kernels, group_forward(): pl.pallas_call(forward_kernel, grid_spec=pltpu.PrefetchScalarGridSpec(num...  15.8 us
    pallas_call x1, Pallas kernels, partials(): pl.pallas_call(partial_kernel, grid_spec=pltpu.PrefetchScalarGridSpec(num...  12.6 us
  transfers between devices with their start and end apart: 5, of which 3 were waited for; matrix products, arithmetic and copies ran while one was open for 1% of the time, Pallas kernels for 20%

profile of v2, /device:TPU:1, one launch (start us, length us, event | category | flops | bytes accessed | tf_op | source)
XLA Modules:
  0.0 449.1 jit_solution(335983045150929196)
XLA Ops:
  7.2 0.0 all-gather.2.cloned.1.call-start
  7.2 0.7 all-gather.2.cloned.1.call-update
  7.9 0.9 convert_reduce_fusion
  8.8 0.7 multiply_add_fusion.slot_ref
  9.5 0.0 copy-start
  9.5 0.8 select_reduce_fusion
  10.3 0.8 all_to_all.9
  11.0 11.5 %all-to-all-start = ((s32[128,1,2]{2,1,0:T(1,128)}), s32[128,1,2]{2,1,0:T(1,128)S(1)}, u32[]{:S(2)}, u32[]{:S(2)}) async-start(s32[128,1,2]{2,1,0:T(1,128)} %bitcast.2), calls=%async_computation | async-start | bytes 131072 | tf_op jit(solution)/shard_map/all_to_all | solution.py:406
  22.5 0.0 copy-done
  22.5 12.6 %shard_map.130 = bf16[256,128,256]{2,1,0:T(8,128)(2,1)} custom-call(s32[112]{0:T(128)} %copy-done, s32[112]{0:T(128)} %src_ref.1, bf16[112,128,128]{2,1,0:T(8,128)(2,1)} %vals_ref.2, bf16[16,128,256]{2,1,0:T(8,128)(2,1)} %bitcast.11), custom_call_target="tpu_custom_call" | custom-call | flops 939524096 | bytes 11010048 | tf_op jit(solution)/shard_map/pallas_call | solution.py:62
  35.1 0.0 all-to-all-done
  35.1 0.5 broadcast.8
  35.6 0.8 reduce.3
  36.4 0.7 reshape.37.refs_0_
  37.1 26.4 %all-gather.2.cloned.1.call-done.table_ref = bf16[128,128,256]{2,1,0:T(8,128)(2,1)} async-done(((bf16[16,128,256]{2,1,0:T(8,128)(2,1)}), bf16[128,128,256]{2,1,0:T(8,128)(2,1)}) %all-gather.2.cloned.1.call-update) | async-done | bytes 8388624 | tf_op jit(solution)/shard_map/all_gather | solution.py:409
  63.6 8.0 %all-to-all-start.1 = ((bf16[128,256,256]{2,1,0:T(8,128)(2,1)}), bf16[128,256,256]{2,1,0:T(8,128)(2,1)}, u32[]{:S(2)}, u32[]{:S(2)}) async-start(bf16[128,256,256]{2,1,0:T(8,128)(2,1)} %bitcast.7), calls=%async_computation.1 | async-start | bytes 33554432 | tf_op jit(solution)/shard_map/all_to_all | solution.py:412
  71.6 0.0 reduce-scatter.5.cloned.1.call-start
  71.7 15.8 %shard_map.131.refs_2_ = f32[16,128,256]{2,1,0:T(8,128)} custom-call(s32[224]{0:T(256)} %refs_0_.3, s32[224]{0:T(256)} %refs_1_.3, bf16[224,128,128]{2,1,0:T(8,128)(2,1)} %refs_2_.3, bf16[128,128,256]{2,1,0:T(8,128)(2,1)} %all-gather.2.cloned.1.call-done.table_ref), custom_call_target="tpu_custom_call" | custom-call | flops 1879048192 | bytes 40000000 | tf_op jit(solution)/shard_map/pallas_call | solution.py:103
  87.5 216.6 %all-to-all-done.1.refs_1_ = bf16[128,256,256]{2,1,0:T(8,128)(2,1)} async-done(((bf16[128,256,256]{2,1,0:T(8,128)(2,1)}), bf16[128,256,256]{2,1,0:T(8,128)(2,1)}, u32[]{:S(2)}, u32[]{:S(2)}) %all-to-all-start.1) | async-done | bytes 16777248 | tf_op jit(solution)/shard_map/all_to_all | solution.py:412
  304.0 19.7 %shard_map.132 = (bf16[2048,256]{1,0:T(8,128)(2,1)}, bf16[2048,256]{1,0:T(8,128)(2,1)}, f32[256,256]{1,0:T(8,128)}) custom-call(s32[256]{0:T(256)} %reshape.37.refs_0_, bf16[128,256,256]{2,1,0:T(8,128)(2,1)} %all-to-all-done.1.refs_1_, f32[16,128,256]{2,1,0:T(8,128)} %shard_map.131.refs_2_, bf16[2048,256]{1,0:T(8,128)(2,1)} %refs_3_.1, ...), custom_call_target="tpu_custom_call" | custom-call | flops 805306368 | bytes 30000000 | tf_op jit(solution)/shard_map/pallas_call | solution.py:190
  323.8 32.2 %shard_map.133 = bf16[64,128,256]{2,1,0:T(8,128)(2,1)} custom-call(s32[224]{0:T(256)} %refs_0_.3, s32[224]{0:T(256)} %refs_1_.3, bf16[224,128,128]{2,1,0:T(8,128)(2,1)} %refs_2_.3, bf16[16,128,256]{2,1,0:T(8,128)(2,1)} %bitcast.8), custom_call_target="tpu_custom_call" | custom-call | flops 939524096 | bytes 20000000 | tf_op jit(solution)/shard_map/pallas_call | solution.py:259
  356.0 0.0 reduce-scatter.5.cloned.1.call-update
  356.0 0.0 reduce-scatter.3.cloned.1.call-start
  356.1 29.1 %shard_map.135 = bf16[64,128,256]{2,1,0:T(8,128)(2,1)} custom-call(s32[224]{0:T(256)} %refs_0_.3, s32[224]{0:T(256)} %refs_1_.3, bf16[224,128,128]{2,1,0:T(8,128)(2,1)} %refs_2_.3, bf16[16,128,256]{2,1,0:T(8,128)(2,1)} %bitcast.9), custom_call_target="tpu_custom_call" | custom-call | flops 939524096 | bytes 20000000 | tf_op jit(solution)/shard_map/pallas_call | solution.py:259
  385.2 0.0 reduce-scatter.3.cloned.1.call-update
  385.2 31.0 %shard_map.134 = f32[256,256]{1,0:T(8,128)} custom-call(f32[256,256]{1,0:T(8,128)} %get-tuple-element.16.refs_0_), custom_call_target="tpu_custom_call" | custom-call | flops 1000000 | bytes 4000000 | tf_op jit(solution)/shard_map/pallas_call | solution.py:353
  416.2 0.0 reduce-scatter.5.cloned.1.call-done
  416.2 22.4 %reduce-scatter.3.cloned.1.call-done = bf16[8,128,256]{2,1,0:T(8,128)(2,1)} async-done(((bf16[64,128,256]{2,1,0:T(8,128)(2,1)}), bf16[8,128,256]{2,1,0:T(8,128)(2,1)}) %reduce-scatter.3.cloned.1.call-update) | async-done | bytes 524304 | tf_op jit(solution)/shard_map/reduce_scatter | solution.py:424
  438.6 2.3 pad_maximum_fusion
  440.9 1.7 copy.17
Async XLA Ops:
  7.2 56.4 %all-gather.2.cloned.1.call-start = ((), (), s32[]{:S(2)}) async-start(), calls=%async_computation.4 | async-start | bytes 9437184 | tf_op jit(solution)/shard_map/all_gather | solution.py:409
  9.5 13.0 %copy-start = (s32[112]{0:T(128)}, s32[112]{0:T(128)S(1)}, u32[]{:S(2)}) copy-start(s32[112]{0:T(128)S(1)} %multiply_add_fusion.slot_ref) | copy-start | bytes 1348
  11.0 24.1 %all-to-all-start = ((s32[128,1,2]{2,1,0:T(1,128)}), s32[128,1,2]{2,1,0:T(1,128)S(1)}, u32[]{:S(2)}, u32[]{:S(2)}) async-start(s32[128,1,2]{2,1,0:T(1,128)} %bitcast.2), calls=%async_computation | async-start | bytes 131072 | tf_op jit(solution)/shard_map/all_to_all | solution.py:406
  63.6 240.5 %all-to-all-start.1 = ((bf16[128,256,256]{2,1,0:T(8,128)(2,1)}), bf16[128,256,256]{2,1,0:T(8,128)(2,1)}, u32[]{:S(2)}, u32[]{:S(2)}) async-start(bf16[128,256,256]{2,1,0:T(8,128)(2,1)} %bitcast.7), calls=%async_computation.1 | async-start | bytes 33554432 | tf_op jit(solution)/shard_map/all_to_all | solution.py:412
  71.6 344.6 %reduce-scatter.5.cloned.1.call-start = ((), (), s32[]{:S(2)}) async-start(), calls=%async_computation.6 | async-start | bytes 4718592 | tf_op jit(solution)/shard_map/reduce_scatter | solution.py:424
  356.0 82.6 %reduce-scatter.3.cloned.1.call-start = ((), (), s32[]{:S(2)}) async-start(), calls=%async_computation.5 | async-start | bytes 4718592 | tf_op jit(solution)/shard_map/reduce_scatter | solution.py:424
Sparse Core Ops, SparseCore 0:
  9.7 53.7 all-gather.1
  356.1 41.1 reduce-scatter.4
  399.7 38.8 reduce-scatter.2

commit v3 on v2

v3 whole, which is shorter than its diff:
```python
import math

import jax
import jax.numpy as jnp
from jax import lax
from jax.experimental import pallas as pl
from jax.experimental.pallas import tpu as pltpu
from jax.sharding import PartitionSpec as P

AXES = ("grp", "mem")
MESH = pl.DeviceIdType.MESH
VMEM_LIMIT = 56 * 1024 * 1024
BATCH = 8


def params(**kw):
    return pltpu.CompilerParams(vmem_limit_bytes=VMEM_LIMIT, **kw)


def full(shape):
    return pl.BlockSpec(shape, lambda *_: (0,) * len(shape))


def cost(flops, moved):
    return pl.CostEstimate(flops=flops, bytes_accessed=moved, transcendentals=0)


def partial_kernel(slot_ref, src_ref, vals_ref, hid_ref, out_ref, stage, sem):
    step = pl.program_id(0)
    half = lax.rem(step, 2)
    per_step = vals_ref.shape[0]

    def drain(which):
        for i in range(per_step):
            pltpu.make_async_copy(stage.at[which, i], out_ref.at[0], sem.at[which, i]).wait()

    @pl.when(step >= 2)
    def _():
        drain(half)

    for i in range(per_step):
        edge = step * per_step + i
        stage[half, i] = jnp.dot(
            vals_ref[i], hid_ref[src_ref[edge]], preferred_element_type=jnp.float32
        ).astype(stage.dtype)
    for i in range(per_step):
        edge = step * per_step + i
        pltpu.make_async_copy(
            stage.at[half, i], out_ref.at[slot_ref[edge]], sem.at[half, i]
        ).start()

    @pl.when(step == pl.num_programs(0) - 1)
    def _():
        drain(1 - half)
        drain(half)


def partials(slot, bnd_src, bnd_vals, blocks, devices):
    count, blk, _ = bnd_vals.shape
    nb, _, feat = blocks.shape
    per_step = 16
    assert count % per_step == 0 and count >= 2 * per_step
    return pl.pallas_call(
        partial_kernel,
        grid_spec=pltpu.PrefetchScalarGridSpec(
            num_scalar_prefetch=2,
            grid=(count // per_step,),
            in_specs=[
                pl.BlockSpec((per_step, blk, blk), lambda i, *_: (i, 0, 0)),
                full(blocks.shape),
            ],
            out_specs=pl.BlockSpec(memory_space=pl.ANY),
            scratch_shapes=[
                pltpu.VMEM((2, per_step, blk, feat), jnp.bfloat16),
                pltpu.SemaphoreType.DMA((2, per_step)),
            ],
        ),
        out_shape=jax.ShapeDtypeStruct((devices * 2, blk, feat), jnp.bfloat16),
        compiler_params=params(),
        cost_estimate=cost(2 * count * blk * blk * feat, 3 * count * blk * feat),
    )(slot, bnd_src, bnd_vals, blocks)


def core_kernel(
    slot_order,
    slot_row,
    filled,
    grp_row,
    grp_col,
    edge_order,
    edge_row,
    edge_col,
    inc_hbm,
    table_hbm,
    vals_hbm,
    initial_hbm,
    cot_hbm,
    w_ref,
    out_hbm,
    term_hbm,
    gw_ref,
    ring,
    table,
    vals,
    initial,
    cot,
    acc,
    out,
    gmix,
    term,
    mixed_all,
    gpre_all,
    mw,
    ring_sem,
    table_sem,
    vals_sem,
    in_sem,
    out_sem,
    term_sem,
):
    nb, blk, feat = gmix.shape
    depth = ring_sem.shape[0] // BATCH
    chunks = vals_sem.shape[0]
    per_chunk = vals.shape[0] // chunks
    batches = (filled[0] + BATCH - 1) // BATCH

    def fetch(batch, i):
        at = lax.rem(batch, depth) * BATCH + i
        return pltpu.make_async_copy(
            inc_hbm.at[slot_order[batch * BATCH + i]], ring.at[at], ring_sem.at[at]
        )

    def fetch_batch(batch):
        @pl.when(batch < batches)
        def _():
            for i in range(BATCH):
                fetch(batch, i).start()

    for batch in range(depth):
        fetch_batch(batch)
    table_copy = pltpu.make_async_copy(table_hbm, table, table_sem)
    table_copy.start()

    def vals_copy(chunk):
        at = pl.ds(chunk * per_chunk, per_chunk)
        return pltpu.make_async_copy(vals_hbm.at[at], vals.at[at], vals_sem.at[chunk])

    def start_vals(chunk, _):
        vals_copy(chunk).start()
        return 0

    lax.fori_loop(0, chunks, start_vals, 0)
    initial_copy = pltpu.make_async_copy(initial_hbm, initial, in_sem.at[0])
    cot_copy = pltpu.make_async_copy(cot_hbm, cot, in_sem.at[1])
    initial_copy.start()
    cot_copy.start()

    def zero_acc(j, _):
        acc[j] = jnp.zeros(acc.shape[1:], acc.dtype)
        return 0

    def zero_term(j, _):
        term[j] = jnp.zeros(term.shape[1:], term.dtype)
        return 0

    lax.fori_loop(0, acc.shape[0], zero_acc, 0)
    lax.fori_loop(0, term.shape[0], zero_term, 0)
    eye = lax.broadcasted_iota(jnp.int32, (feat, feat), 0) == lax.broadcasted_iota(
        jnp.int32, (feat, feat), 1
    )
    mw[...] = (
        jnp.where(eye, 0.5, 0.0).astype(jnp.float32) + 0.5 * w_ref[...].astype(jnp.float32)
    ).astype(jnp.bfloat16)

    def add_batch(batch, _):
        for i in range(BATCH):
            fetch(batch, i).wait()
        for i in range(BATCH):
            at = lax.rem(batch, depth) * BATCH + i
            acc[slot_row[batch * BATCH + i]] += ring[at].astype(jnp.float32)
        fetch_batch(batch + depth)
        return 0

    lax.fori_loop(0, batches, add_batch, 0)
    table_copy.wait()

    def forward(chunk, _):
        vals_copy(chunk).wait()
        for i in range(per_chunk):
            b = chunk * per_chunk + i
            acc[grp_row[b]] += jnp.dot(
                vals[b], table[grp_col[b]], preferred_element_type=jnp.float32
            )
        return 0

    lax.fori_loop(0, chunks, forward, 0)
    initial_copy.wait()
    cot_copy.wait()
    wide = 4

    def dense(j, _):
        at = pl.ds(pl.multiple_of(j * wide * blk, wide * blk), wide * blk)
        summed = acc[pl.ds(j * wide, wide)].reshape(wide * blk, feat)
        mixed = (0.9 * summed + 0.1 * initial[at, :].astype(jnp.float32)).astype(jnp.bfloat16)
        pre = jnp.dot(mixed, mw[...], preferred_element_type=jnp.float32)
        sig = jax.nn.sigmoid(pre)
        out[at, :] = (pre * sig).astype(jnp.bfloat16)
        gpre = (cot[at, :].astype(jnp.float32) * sig * (1.0 + pre * (1.0 - sig))).astype(
            jnp.bfloat16
        )
        mixed_all[at, :] = mixed
        gpre_all[at, :] = gpre
        gmix[pl.ds(j * wide, wide)] = (
            lax.dot_general(
                gpre, mw[...], (((1,), (1,)), ((), ())), preferred_element_type=jnp.float32
            )
            .astype(jnp.bfloat16)
            .reshape(wide, blk, feat)
        )
        return 0

    lax.fori_loop(0, nb // wide, dense, 0)
    out_copy = pltpu.make_async_copy(out, out_hbm, out_sem)
    out_copy.start()
    gw_ref[...] = lax.dot_general(
        mixed_all[...], gpre_all[...], (((0,), (0,)), ((), ())), preferred_element_type=jnp.float32
    )

    def send_term(c, _):
        pltpu.make_async_copy(term.at[c], term_hbm.at[c], term_sem).start()
        return 0

    running = acc.at[0]
    running[...] = jnp.zeros((blk, feat), jnp.float32)

    def backward(chunk, sent):
        total = running[...]
        for i in range(per_chunk):
            b = chunk * per_chunk + i
            col = edge_col[b]
            same = (col == edge_col[jnp.maximum(b - 1, 0)]).astype(jnp.float32)
            total = total * same + lax.dot_general(
                vals[edge_order[b]],
                gmix[edge_row[b]],
                (((0,), (0,)), ((), ())),
                preferred_element_type=jnp.float32,
            )
            term[col] = (0.9 * total).astype(term.dtype)
        running[...] = total
        past = edge_col[chunk * per_chunk + per_chunk - 1]
        lax.fori_loop(sent, past, send_term, 0)
        return past

    sent = lax.fori_loop(0, chunks, backward, jnp.int32(0))
    lax.fori_loop(sent, term.shape[0], send_term, 0)
    out_copy.wait()
    pltpu.make_async_copy(term, term_hbm, term_sem).wait()


def core(scalars, incoming, table, grp_vals, initial, cotangent, weight, nb):
    count, blk, _ = grp_vals.shape
    nodes, feat = initial.shape
    ring, chunks = 4 * BATCH, 7
    assert count % chunks == 0 and incoming.shape[0] % BATCH == 0
    smem = pl.BlockSpec(memory_space=pltpu.SMEM)
    hbm = pl.BlockSpec(memory_space=pl.ANY)
    vmem = pl.BlockSpec(memory_space=pltpu.VMEM)
    bf16, dma = jnp.bfloat16, pltpu.SemaphoreType.DMA
    return pl.pallas_call(
        core_kernel,
        in_specs=[smem] * len(scalars) + [hbm] * 5 + [vmem],
        out_specs=[hbm, hbm, vmem],
        out_shape=[
            jax.ShapeDtypeStruct((nodes, feat), bf16),
            jax.ShapeDtypeStruct(table.shape, bf16),
            jax.ShapeDtypeStruct((feat, feat), jnp.float32),
        ],
        scratch_shapes=[
            pltpu.VMEM((ring, blk, feat), bf16),
            pltpu.VMEM(table.shape, bf16),
            pltpu.VMEM(grp_vals.shape, bf16),
            pltpu.VMEM((nodes, feat), bf16),
            pltpu.VMEM((nodes, feat), bf16),
            pltpu.VMEM((nb + 1, blk, feat), jnp.float32),
            pltpu.VMEM((nodes, feat), bf16),
            pltpu.VMEM((nb, blk, feat), bf16),
            pltpu.VMEM(table.shape, bf16),
            pltpu.VMEM((nodes, feat), bf16),
            pltpu.VMEM((nodes, feat), bf16),
            pltpu.VMEM((feat, feat), bf16),
            dma((ring,)),
            dma,
            dma((chunks,)),
            dma((2,)),
            dma,
            dma,
        ],
        compiler_params=params(),
        cost_estimate=cost(4 * count * blk * blk * feat + 6 * nodes * feat * feat, 60_000_000),
    )(*scalars, incoming, table, grp_vals, initial, cotangent, weight)


def reduce_kernel(groups, members, scale, x_ref, out_ref, part, whole, done, sems):
    g, m = lax.axis_index("grp"), lax.axis_index("mem")
    rows = part.shape[1]
    barrier = pltpu.get_barrier_semaphore()
    mates = [lax.rem(m + k, members) for k in range(1, members)]
    peers = [lax.rem(g + k, groups) for k in range(1, groups)]
    for mate in mates:
        pl.semaphore_signal(barrier, inc=1, device_id=(g, mate), device_id_type=MESH)
    for peer in peers:
        pl.semaphore_signal(barrier, inc=1, device_id=(peer, m), device_id_type=MESH)
    pl.semaphore_wait(barrier, members + groups - 2)

    def exchange(stage, targets, source, target):
        copies = []
        for k, (device, src) in enumerate(zip(targets, source)):
            copies.append(
                pltpu.make_async_remote_copy(
                    src,
                    target,
                    sems.at[2 * stage, k],
                    sems.at[2 * stage + 1, k],
                    device_id=device,
                    device_id_type=MESH,
                )
            )
            copies[-1].start()
        return copies

    def at(index):
        return pl.ds(pl.multiple_of(index * rows, rows), rows)

    def total(buffer):
        result = buffer[0]
        for k in range(1, buffer.shape[0]):
            result = result + buffer[k]
        return result

    far = [(peer, m) for peer in peers]
    copies = exchange(0, far, [x_ref.at[at(peer)] for peer in peers], part.at[g])
    part[g] = x_ref[at(g), :]
    for copy in copies:
        copy.wait()
    whole[m] = total(part)
    for copy in exchange(1, [(g, mate) for mate in mates], [whole.at[m]] * len(mates), whole.at[m]):
        copy.wait()
    done[g] = total(whole) * scale
    for copy in exchange(2, far, [done.at[g]] * len(far), done.at[g]):
        copy.wait()
    for k in range(groups):
        out_ref[k * rows : (k + 1) * rows, :] = done[k]


def all_reduce(x, scale, groups, members):
    rows, cols = x.shape
    share = rows // groups
    return pl.pallas_call(
        lambda *refs: reduce_kernel(groups, members, scale, *refs),
        out_shape=jax.ShapeDtypeStruct(x.shape, x.dtype),
        in_specs=[pl.BlockSpec(memory_space=pltpu.VMEM)],
        out_specs=pl.BlockSpec(memory_space=pltpu.VMEM),
        scratch_shapes=[
            pltpu.VMEM((groups, share, cols), jnp.float32),
            pltpu.VMEM((members, share, cols), jnp.float32),
            pltpu.VMEM((groups, share, cols), jnp.float32),
            pltpu.SemaphoreType.DMA((6, max(groups, members) - 1)),
        ],
        compiler_params=params(collective_id=0, has_side_effects=True),
        cost_estimate=cost(1_000_000, 4_000_000),
    )(x)


def sorted_by(key, *values):
    ids = jnp.arange(key.shape[0], dtype=jnp.int32)
    ahead = (key[None, :] < key[:, None]) | (
        (key[None, :] == key[:, None]) & (ids[None, :] < ids[:, None])
    )
    rank = jnp.sum(ahead, axis=1, dtype=jnp.int32)
    hit = rank[None, :] == ids[:, None]
    return [jnp.sum(jnp.where(hit, value[None, :], 0), axis=1) for value in (ids, *values)]


def per_device(
    hidden,
    initial,
    weight,
    grp_vals,
    grp_row,
    grp_col,
    bnd_vals,
    bnd_src,
    bnd_dst,
    bnd_row,
    cotangent,
):
    blk = grp_vals.shape[1]
    nodes, feat = hidden.shape
    nb = nodes // blk
    devices = lax.axis_size(AXES)
    groups, members = lax.axis_size("grp"), lax.axis_size("mem")
    count = bnd_vals.shape[0]
    blocks = hidden.reshape(nb, blk, feat)

    target = bnd_dst[:, 0]
    ids = jnp.arange(count, dtype=jnp.int32)
    place = jnp.sum(
        (target[:, None] == target[None, :]) & (ids[None, :] < ids[:, None]),
        axis=1,
        dtype=jnp.int32,
    )
    slot = target * 2 + place
    out_rows = jnp.max(
        jnp.where(
            slot[None, :] == jnp.arange(2 * devices, dtype=jnp.int32)[:, None],
            bnd_row[None, :],
            -1,
        ),
        axis=1,
    )
    in_rows = lax.all_to_all(
        out_rows.reshape(devices, 2), AXES, split_axis=0, concat_axis=0, tiled=True
    ).reshape(-1)
    table = lax.all_gather(blocks, "mem", axis=0, tiled=True)
    outgoing = partials(slot, bnd_src, bnd_vals, blocks, devices)
    outgoing, grp_row, grp_col = lax.optimization_barrier((outgoing, grp_row, grp_col))
    incoming = lax.all_to_all(
        outgoing.reshape(devices, 2 * blk, feat), AXES, split_axis=0, concat_axis=0, tiled=True
    )
    edge_order, edge_row, edge_col = sorted_by(grp_col, grp_row, grp_col)
    empty = in_rows < 0
    slot_order, slot_row = sorted_by(
        empty.astype(jnp.int32), jnp.where(empty, nb, in_rows)
    )
    filled = jnp.sum(~empty, dtype=jnp.int32)[None]
    output, term, local_weight = core(
        (slot_order, slot_row, filled, grp_row, grp_col, edge_order, edge_row, edge_col),
        incoming.reshape(2 * devices, blk, feat),
        table,
        grp_vals,
        initial,
        cotangent,
        weight,
        nb,
    )
    grad_hidden = lax.psum_scatter(term, "mem", scatter_dimension=0, tiled=True)
    grad_weight = all_reduce(local_weight, 0.5 / math.sqrt(nodes * devices), groups, members)
    return output, grad_weight, grad_hidden.reshape(nodes, feat)


def solution(mesh):
    return jax.shard_map(
        per_device,
        mesh=mesh,
        in_specs=(
            P(AXES, None),
            P(AXES, None),
            P(),
            P(AXES, None, None),
            P(AXES),
            P(AXES),
            P(AXES, None, None),
            P(AXES),
            P(AXES, None),
            P(AXES),
            P(AXES, None),
        ),
        out_specs=(P(AXES, None), P(), P(AXES, None)),
        check_vma=False,
    )
```

time: 452 us -> 376 us (0.83)
  Pallas kernels: 140 us -> 72.7 us
  waiting for transfers between devices: 266 us -> 257 us
    all_to_all x1, waiting for transfers between devices: 217 us -> 7.42 us  [per_device(): lax.all_to_all(outgoing.reshape(devices, 2 * blk, feat), AXES, split_axis...]
    all_gather x1, waiting for transfers between devices: 26.4 us -> 219 us  [per_device(): table = lax.all_gather(blocks, 'mem', axis=0, tiled=True)]
    pallas_call x4 -> x1, Pallas kernels: 96.9 us -> 25.6 us  [core(): pl.pallas_call(core_kernel, in_specs=[smem] * len(scalars) + [hbm] * 5 +...]
    reduce_scatter x2 -> x1, waiting for transfers between devices: 22.4 us -> 29.6 us  [per_device(): grad_hidden = lax.psum_scatter(term, 'mem', scatter_dimension=0, tiled=True)]
    pallas_call x1, Pallas kernels: 31 us -> 37.7 us  [all_reduce(): pl.pallas_call(lambda *refs: reduce_kernel(groups, members, scale, *refs)...]
  transfers between devices with their start and end apart: 5 -> 4, of which waited for: 3 -> 3; matrix products, arithmetic and copies ran while one was open for 1% -> 1% of each run, Pallas kernels for 20% -> 13%
where the time goes in v3:
time: 376 us; the launch traced here: 375 us
  waiting for transfers between devices  257 us (68%)
  Pallas kernels  72.7 us (19%)
  starting transfers between devices  21.8 us (6%)
  between operations  14.2 us (4%)
  other arithmetic  5.79 us (2%)
    all_gather x1, waiting for transfers between devices, per_device(): table = lax.all_gather(blocks, 'mem', axis=0, tiled=True)  219 us
    pallas_call x1, Pallas kernels, all_reduce(): pl.pallas_call(lambda *refs: reduce_kernel(groups, members, scale, *refs)...  37.7 us
    reduce_scatter x1, waiting for transfers between devices, per_device(): grad_hidden = lax.psum_scatter(term, 'mem', scatter_dimension=0, tiled=True)  29.6 us
    pallas_call x1, Pallas kernels, core(): pl.pallas_call(core_kernel, in_specs=[smem] * len(scalars) + [hbm] * 5 +...  25.6 us
    all_to_all x1, starting transfers between devices, per_device(): lax.all_to_all(out_rows.reshape(devices, 2), AXES, split_axis=0, concat_a...  11.5 us
    all_to_all x1, starting transfers between devices, per_device(): lax.all_to_all(outgoing.reshape(devices, 2 * blk, feat), AXES, split_axis...  10.2 us
    pallas_call x1, Pallas kernels, partials(): pl.pallas_call(partial_kernel, grid_spec=pltpu.PrefetchScalarGridSpec(num...  9.44 us
  transfers between devices with their start and end apart: 4, of which 3 were waited for; matrix products, arithmetic and copies ran while one was open for 1% of the time, Pallas kernels for 13%

profile of v3, /device:TPU:1, one launch (start us, length us, event | category | flops | bytes accessed | tf_op | source)
XLA Modules:
  0.0 374.7 jit_solution(9118051690499796958)
XLA Ops:
  7.2 0.9 convert_reduce_fusion.2
  8.1 0.7 multiply_add_fusion.slot_ref
  8.7 0.0 copy-start.2
  8.8 0.8 select_reduce_fusion.5
  9.5 0.8 all_to_all.9
  10.3 11.5 %all-to-all-start = ((s32[128,1,2]{2,1,0:T(1,128)}), s32[128,1,2]{2,1,0:T(1,128)S(1)}, u32[]{:S(2)}, u32[]{:S(2)}) async-start(s32[128,1,2]{2,1,0:T(1,128)} %bitcast.1), calls=%async_computation | async-start | bytes 131072 | tf_op jit(solution)/shard_map/all_to_all | solution.py:421
  21.8 0.0 copy-done.2
  21.8 9.4 %shard_map.130 = bf16[256,128,256]{2,1,0:T(8,128)(2,1)} custom-call(s32[112]{0:T(128)} %copy-done.2, s32[112]{0:T(128)} %src_ref.1, bf16[112,128,128]{2,1,0:T(8,128)(2,1)} %vals_ref.1, bf16[16,128,256]{2,1,0:T(8,128)(2,1)} %bitcast.9), custom_call_target="tpu_custom_call" | custom-call | flops 939524096 | bytes 11010048 | tf_op jit(solution)/shard_map/pallas_call | solution.py:63
  31.3 0.0 all-to-all-done
  31.3 0.0 copy-start
  31.3 0.0 copy-start.1
  31.3 10.2 %all-to-all-start.1 = ((bf16[128,256,256]{2,1,0:T(8,128)(2,1)}), bf16[128,256,256]{2,1,0:T(8,128)(2,1)}, u32[]{:S(2)}, u32[]{:S(2)}) async-start(bf16[128,256,256]{2,1,0:T(8,128)(2,1)} %bitcast.8), calls=%async_computation.1 | async-start | bytes 33554432 | tf_op jit(solution)/shard_map/all_to_all | solution.py:427
  41.5 0.0 all-gather.2.cloned.1.call-start
  41.6 0.7 all-gather.2.cloned.1.call-update
  42.3 0.0 reduce-scatter.2.cloned.1.call-start
  42.3 0.0 copy-done
  42.3 0.2 convert_reduce_fusion.1
  42.5 0.0 copy-done.1
  42.5 0.8 select_reduce_fusion.2
  43.3 0.5 broadcast.31
  43.8 0.8 reduce.5
  44.6 0.1 reshape.66
  44.8 0.1 copy.17
  44.8 0.7 fusion.5
  45.5 0.2 convert_reduce_fusion
  45.8 0.7 select_reduce_fusion
  46.5 219.3 %all-gather.2.cloned.1.call-done.table_hbm = bf16[128,128,256]{2,1,0:T(8,128)(2,1)} async-done(((bf16[16,128,256]{2,1,0:T(8,128)(2,1)}), bf16[128,128,256]{2,1,0:T(8,128)(2,1)}) %all-gather.2.cloned.1.call-update) | async-done | bytes 8388624 | tf_op jit(solution)/shard_map/all_gather | solution.py:424
  265.8 7.4 %all-to-all-done.1 = bf16[128,256,256]{2,1,0:T(8,128)(2,1)} async-done(((bf16[128,256,256]{2,1,0:T(8,128)(2,1)}), bf16[128,256,256]{2,1,0:T(8,128)(2,1)}, u32[]{:S(2)}, u32[]{:S(2)}) %all-to-all-start.1) | async-done | bytes 16777248 | tf_op jit(solution)/shard_map/all_to_all | solution.py:427
  273.2 25.6 %shard_map.131 = (bf16[2048,256]{1,0:T(8,128)(2,1)}, bf16[128,128,256]{2,1,0:T(8,128)(2,1)}, f32[256,256]{1,0:T(8,128)}) custom-call(s32[256]{0:T(256)} %get-tuple-element.19.slot_order, s32[256]{0:T(256)} %get-tuple-element.18.slot_row, s32[1]{0:T(128)} %bitcast.2.filled, s32[224]{0:T(256)} %grp_row, s32[224]{0:T(256)} %grp_col, ...), custom_call_target="tpu_custom_call" | custom-call | flops 4563402752 | bytes 60000000 | tf_op jit(solution)/shard_map/pallas_call | solution.py:269
  298.8 0.0 reduce-scatter.2.cloned.1.call-update
  298.8 37.7 %shard_map.132 = f32[256,256]{1,0:T(8,128)} custom-call(f32[256,256]{1,0:T(8,128)} %get-tuple-element.13.refs_0_), custom_call_target="tpu_custom_call" | custom-call | flops 1000000 | bytes 4000000 | tf_op jit(solution)/shard_map/pallas_call | solution.py:358
  336.5 29.6 %reduce-scatter.2.cloned.1.call-done = bf16[16,128,256]{2,1,0:T(8,128)(2,1)} async-done(((bf16[128,128,256]{2,1,0:T(8,128)(2,1)}), bf16[16,128,256]{2,1,0:T(8,128)(2,1)}) %reduce-scatter.2.cloned.1.call-update) | async-done | bytes 1048592 | tf_op jit(solution)/shard_map/reduce_scatter | solution.py:446
  366.2 1.7 copy.19
  (2 shorter events, 0.0 us)
Async XLA Ops:
  8.7 13.0 %copy-start.2 = (s32[112]{0:T(128)}, s32[112]{0:T(128)S(1)}, u32[]{:S(2)}) copy-start(s32[112]{0:T(128)S(1)} %multiply_add_fusion.slot_ref) | copy-start | bytes 1348
  10.3 21.0 %all-to-all-start = ((s32[128,1,2]{2,1,0:T(1,128)}), s32[128,1,2]{2,1,0:T(1,128)S(1)}, u32[]{:S(2)}, u32[]{:S(2)}) async-start(s32[128,1,2]{2,1,0:T(1,128)} %bitcast.1), calls=%async_computation | async-start | bytes 131072 | tf_op jit(solution)/shard_map/all_to_all | solution.py:421
  31.3 11.0 %copy-start = (s32[224]{0:T(256)S(1)}, s32[224]{0:T(256)}, u32[]{:S(2)}) copy-start(s32[224]{0:T(256)} %grp_col) | copy-start | bytes 2692
  31.3 11.2 %copy-start.1 = (s32[224]{0:T(256)S(1)}, s32[224]{0:T(256)}, u32[]{:S(2)}) copy-start(s32[224]{0:T(256)} %grp_row) | copy-start | bytes 2692
  31.3 241.9 %all-to-all-start.1 = ((bf16[128,256,256]{2,1,0:T(8,128)(2,1)}), bf16[128,256,256]{2,1,0:T(8,128)(2,1)}, u32[]{:S(2)}, u32[]{:S(2)}) async-start(bf16[128,256,256]{2,1,0:T(8,128)(2,1)} %bitcast.8), calls=%async_computation.1 | async-start | bytes 33554432 | tf_op jit(solution)/shard_map/all_to_all | solution.py:427
  41.5 224.3 %all-gather.2.cloned.1.call-start = ((), (), s32[]{:S(2)}) async-start(), calls=%async_computation.3 | async-start | bytes 9437184 | tf_op jit(solution)/shard_map/all_gather | solution.py:424
  42.3 323.9 %reduce-scatter.2.cloned.1.call-start = ((), (), s32[]{:S(2)}) async-start(), calls=%async_computation.4 | async-start | bytes 9437184 | tf_op jit(solution)/shard_map/reduce_scatter | solution.py:446
Sparse Core Ops, SparseCore 0:
  44.1 221.6 all-gather.1
  299.0 67.1 reduce-scatter.1

commit v4 on v3

--- a/solution.py
+++ b/solution.py
@@ -423,18 +423,19 @@
     ).reshape(-1)
     table = lax.all_gather(blocks, "mem", axis=0, tiled=True)
     outgoing = partials(slot, bnd_src, bnd_vals, blocks, devices)
-    outgoing, grp_row, grp_col = lax.optimization_barrier((outgoing, grp_row, grp_col))
-    incoming = lax.all_to_all(
-        outgoing.reshape(devices, 2 * blk, feat), AXES, split_axis=0, concat_axis=0, tiled=True
-    )
     edge_order, edge_row, edge_col = sorted_by(grp_col, grp_row, grp_col)
     empty = in_rows < 0
     slot_order, slot_row = sorted_by(
         empty.astype(jnp.int32), jnp.where(empty, nb, in_rows)
     )
     filled = jnp.sum(~empty, dtype=jnp.int32)[None]
+    scalars = (slot_order, slot_row, filled, grp_row, grp_col, edge_order, edge_row, edge_col)
+    outgoing, table, scalars = lax.optimization_barrier((outgoing, table, scalars))
+    incoming = lax.all_to_all(
+        outgoing.reshape(devices, 2 * blk, feat), AXES, split_axis=0, concat_axis=0, tiled=True
+    )
     output, term, local_weight = core(
-        (slot_order, slot_row, filled, grp_row, grp_col, edge_order, edge_row, edge_col),
+        scalars,
         incoming.reshape(2 * devices, blk, feat),
         table,
         grp_vals,

time: 376 us -> 357 us (0.949)
  waiting for transfers between devices: 257 us -> 55.3 us
  blocking collectives: 0 us -> 197 us
  starting transfers between devices: 21.8 us -> 11.6 us
  Pallas kernels: 72.7 us -> 67.7 us
    all_to_all x0 -> x1, blocking collectives: none -> 197 us  [per_device(): lax.all_to_all(outgoing.reshape(devices, 2 * blk, feat), AXES, split_axis...]
    all_gather x1, waiting for transfers between devices: 219 us -> 25.9 us  [per_device(): table = lax.all_gather(blocks, 'mem', axis=0, tiled=True)]
    all_to_all x1 -> x0, starting transfers between devices: 10.2 us -> none  [per_device(): lax.all_to_all(outgoing.reshape(devices, 2 * blk, feat), AXES, split_axis...]
    all_to_all x1 -> x0, waiting for transfers between devices: 7.42 us -> none  [per_device(): lax.all_to_all(outgoing.reshape(devices, 2 * blk, feat), AXES, split_axis...]
    pallas_call x1, Pallas kernels: 37.7 us -> 32.7 us  [all_reduce(): pl.pallas_call(lambda *refs: reduce_kernel(groups, members, scale, *refs)...]
  transfers between devices with their start and end apart: 4 -> 3, of which waited for: 3 -> 2; matrix products, arithmetic and copies ran while one was open for 1% -> 2% of each run, Pallas kernels for 13% -> 12%
where the time goes in v4:
time: 357 us; the launch traced here: 356 us
  blocking collectives  197 us (55%)
  Pallas kernels  67.7 us (19%)
  waiting for transfers between devices  55.3 us (15%)
  between operations  14.1 us (4%)
  starting transfers between devices  11.6 us (3%)
  other arithmetic  7.23 us (2%)
    all_to_all x1, blocking collectives, per_device(): lax.all_to_all(outgoing.reshape(devices, 2 * blk, feat), AXES, split_axis...  197 us
    pallas_call x1, Pallas kernels, all_reduce(): pl.pallas_call(lambda *refs: reduce_kernel(groups, members, scale, *refs)...  32.7 us
    reduce_scatter x1, waiting for transfers between devices, per_device(): grad_hidden = lax.psum_scatter(term, 'mem', scatter_dimension=0, tiled=True)  28.7 us
    all_gather x1, waiting for transfers between devices, per_device(): table = lax.all_gather(blocks, 'mem', axis=0, tiled=True)  25.9 us
    pallas_call x1, Pallas kernels, core(): pl.pallas_call(core_kernel, in_specs=[smem] * len(scalars) + [hbm] * 5 +...  25.6 us
    all_to_all x1, starting transfers between devices, per_device(): lax.all_to_all(out_rows.reshape(devices, 2), AXES, split_axis=0, concat_a...  11.5 us
    pallas_call x1, Pallas kernels, partials(): pl.pallas_call(partial_kernel, grid_spec=pltpu.PrefetchScalarGridSpec(num...  9.46 us
  transfers between devices with their start and end apart: 3, of which 2 were waited for; matrix products, arithmetic and copies ran while one was open for 2% of the time, Pallas kernels for 12%

profile of v4, /device:TPU:1, one launch (start us, length us, event | category | flops | bytes accessed | tf_op | source)
XLA Modules:
  0.0 356.1 jit_solution(9932725837260602584)
XLA Ops:
  7.2 0.0 all-gather.2.cloned.1.call-start
  7.2 0.7 all-gather.2.cloned.1.call-update
  7.9 0.9 convert_reduce_fusion.2
  8.8 0.7 multiply_add_fusion.slot_ref
  9.5 0.0 copy-start
  9.5 0.8 select_reduce_fusion.5
  10.3 0.8 all_to_all.9
  11.0 11.5 %all-to-all-start = ((s32[128,1,2]{2,1,0:T(1,128)}), s32[128,1,2]{2,1,0:T(1,128)S(1)}, u32[]{:S(2)}, u32[]{:S(2)}) async-start(s32[128,1,2]{2,1,0:T(1,128)} %bitcast.2), calls=%async_computation | async-start | bytes 131072 | tf_op jit(solution)/shard_map/all_to_all | solution.py:421
  22.5 0.0 reduce-scatter.2.cloned.1.call-start
  22.6 0.9 convert_reduce_fusion.1
  23.5 1.5 select_reduce_fusion.2
  25.0 0.0 copy-done
  25.0 9.5 %shard_map.130 = bf16[256,128,256]{2,1,0:T(8,128)(2,1)} custom-call(s32[112]{0:T(128)} %copy-done, s32[112]{0:T(128)} %src_ref.1, bf16[112,128,128]{2,1,0:T(8,128)(2,1)} %vals_ref.1, bf16[16,128,256]{2,1,0:T(8,128)(2,1)} %bitcast.11), custom_call_target="tpu_custom_call" | custom-call | flops 939524096 | bytes 11010048 | tf_op jit(solution)/shard_map/pallas_call | solution.py:63
  34.5 0.0 all-to-all-done
  34.5 0.5 broadcast.31
  35.0 0.8 reduce.5
  35.8 0.1 reshape.67
  36.0 0.1 copy.17
  36.0 0.7 fusion.5
  36.7 0.2 convert_reduce_fusion
  36.9 0.7 select_reduce_fusion
  37.7 25.9 %all-gather.2.cloned.1.call-done.table_hbm = bf16[128,128,256]{2,1,0:T(8,128)(2,1)} async-done(((bf16[16,128,256]{2,1,0:T(8,128)(2,1)}), bf16[128,128,256]{2,1,0:T(8,128)(2,1)}) %all-gather.2.cloned.1.call-update) | async-done | bytes 8388624 | tf_op jit(solution)/shard_map/all_gather | solution.py:424
  63.6 196.9 %all_to_all.14 = bf16[128,256,256]{2,1,0:T(8,128)(2,1)} all-to-all(bf16[128,256,256]{2,1,0:T(8,128)(2,1)} %bitcast.8), channel_id=1, replica_groups=mesh['grp'=16,'mem'=8] {'grp','mem'}, dimensions={0} | all-to-all | bytes 33554432 | tf_op jit(solution)/shard_map/all_to_all | solution.py:434
  260.5 25.6 %shard_map.131 = (bf16[2048,256]{1,0:T(8,128)(2,1)}, bf16[128,128,256]{2,1,0:T(8,128)(2,1)}, f32[256,256]{1,0:T(8,128)}) custom-call(s32[256]{0:T(256)} %get-tuple-element.16.slot_order, s32[256]{0:T(256)} %get-tuple-element.17.slot_row, s32[1]{0:T(128)} %bitcast.3.filled, s32[224]{0:T(256)} %grp_row, s32[224]{0:T(256)} %grp_col, ...), custom_call_target="tpu_custom_call" | custom-call | flops 4563402752 | bytes 60000000 | tf_op jit(solution)/shard_map/pallas_call | solution.py:269
  286.1 0.0 reduce-scatter.2.cloned.1.call-update
  286.1 32.7 %shard_map.132 = f32[256,256]{1,0:T(8,128)} custom-call(f32[256,256]{1,0:T(8,128)} %get-tuple-element.27.refs_0_), custom_call_target="tpu_custom_call" | custom-call | flops 1000000 | bytes 4000000 | tf_op jit(solution)/shard_map/pallas_call | solution.py:358
  318.8 28.7 %reduce-scatter.2.cloned.1.call-done = bf16[16,128,256]{2,1,0:T(8,128)(2,1)} async-done(((bf16[128,128,256]{2,1,0:T(8,128)(2,1)}), bf16[16,128,256]{2,1,0:T(8,128)(2,1)}) %reduce-scatter.2.cloned.1.call-update) | async-done | bytes 1048592 | tf_op jit(solution)/shard_map/reduce_scatter | solution.py:447
  347.6 1.7 copy.19
  (2 shorter events, 0.0 us)
Async XLA Ops:
  7.2 56.4 %all-gather.2.cloned.1.call-start = ((), (), s32[]{:S(2)}) async-start(), calls=%async_computation.3 | async-start | bytes 9437184 | tf_op jit(solution)/shard_map/all_gather | solution.py:424
  9.5 15.5 %copy-start = (s32[112]{0:T(128)}, s32[112]{0:T(128)S(1)}, u32[]{:S(2)}) copy-start(s32[112]{0:T(128)S(1)} %multiply_add_fusion.slot_ref) | copy-start | bytes 1348
  11.0 23.5 %all-to-all-start = ((s32[128,1,2]{2,1,0:T(1,128)}), s32[128,1,2]{2,1,0:T(1,128)S(1)}, u32[]{:S(2)}, u32[]{:S(2)}) async-start(s32[128,1,2]{2,1,0:T(1,128)} %bitcast.2), calls=%async_computation | async-start | bytes 131072 | tf_op jit(solution)/shard_map/all_to_all | solution.py:421
  22.5 325.0 %reduce-scatter.2.cloned.1.call-start = ((), (), s32[]{:S(2)}) async-start(), calls=%async_computation.4 | async-start | bytes 9437184 | tf_op jit(solution)/shard_map/reduce_scatter | solution.py:447
Sparse Core Ops, SparseCore 0:
  9.7 53.7 all-gather.1
  286.2 61.2 reduce-scatter.1

commit v5 on v4

--- a/solution.py
+++ b/solution.py
@@ -105,6 +105,7 @@
     initial,
     cot,
     acc,
+    running,
     out,
     gmix,
     term,
@@ -163,7 +164,7 @@
         term[j] = jnp.zeros(term.shape[1:], term.dtype)
         return 0
 
-    lax.fori_loop(0, acc.shape[0], zero_acc, 0)
+    lax.fori_loop(0, nb, zero_acc, 0)
     lax.fori_loop(0, term.shape[0], zero_term, 0)
     eye = lax.broadcasted_iota(jnp.int32, (feat, feat), 0) == lax.broadcasted_iota(
         jnp.int32, (feat, feat), 1
@@ -172,15 +173,24 @@
         jnp.where(eye, 0.5, 0.0).astype(jnp.float32) + 0.5 * w_ref[...].astype(jnp.float32)
     ).astype(jnp.bfloat16)
 
+    def follows(key, at):
+        return (key[at] == key[jnp.maximum(at - 1, 0)]).astype(jnp.float32)
+
     def add_batch(batch, _):
         for i in range(BATCH):
             fetch(batch, i).wait()
+        total = running[...]
         for i in range(BATCH):
-            at = lax.rem(batch, depth) * BATCH + i
-            acc[slot_row[batch * BATCH + i]] += ring[at].astype(jnp.float32)
+            at = batch * BATCH + i
+            total = total * follows(slot_row, at) + ring[
+                lax.rem(batch, depth) * BATCH + i
+            ].astype(jnp.float32)
+            acc[slot_row[at]] = total
+        running[...] = total
         fetch_batch(batch + depth)
         return 0
 
+    running[...] = jnp.zeros_like(running)
     lax.fori_loop(0, batches, add_batch, 0)
     table_copy.wait()
 
@@ -230,16 +240,14 @@
         pltpu.make_async_copy(term.at[c], term_hbm.at[c], term_sem).start()
         return 0
 
-    running = acc.at[0]
-    running[...] = jnp.zeros((blk, feat), jnp.float32)
+    running[...] = jnp.zeros_like(running)
 
     def backward(chunk, sent):
         total = running[...]
         for i in range(per_chunk):
             b = chunk * per_chunk + i
             col = edge_col[b]
-            same = (col == edge_col[jnp.maximum(b - 1, 0)]).astype(jnp.float32)
-            total = total * same + lax.dot_general(
+            total = total * follows(edge_col, b) + lax.dot_general(
                 vals[edge_order[b]],
                 gmix[edge_row[b]],
                 (((0,), (0,)), ((), ())),
@@ -260,7 +268,7 @@
 def core(scalars, incoming, table, grp_vals, initial, cotangent, weight, nb):
     count, blk, _ = grp_vals.shape
     nodes, feat = initial.shape
-    ring, chunks = 4 * BATCH, 7
+    ring, chunks = 16 * BATCH, 7
     assert count % chunks == 0 and incoming.shape[0] % BATCH == 0
     smem = pl.BlockSpec(memory_space=pltpu.SMEM)
     hbm = pl.BlockSpec(memory_space=pl.ANY)
@@ -282,6 +290,7 @@
             pltpu.VMEM((nodes, feat), bf16),
             pltpu.VMEM((nodes, feat), bf16),
             pltpu.VMEM((nb + 1, blk, feat), jnp.float32),
+            pltpu.VMEM((blk, feat), jnp.float32),
             pltpu.VMEM((nodes, feat), bf16),
             pltpu.VMEM((nb, blk, feat), bf16),
             pltpu.VMEM(table.shape, bf16),
@@ -300,7 +309,7 @@
     )(*scalars, incoming, table, grp_vals, initial, cotangent, weight)
 
 
-def reduce_kernel(groups, members, scale, x_ref, out_ref, part, whole, done, sems):
+def reduce_kernel(groups, members, x_ref, out_ref, part, whole, done, sems):
     g, m = lax.axis_index("grp"), lax.axis_index("mem")
     rows = part.shape[1]
     barrier = pltpu.get_barrier_semaphore()
@@ -345,18 +354,18 @@
     whole[m] = total(part)
     for copy in exchange(1, [(g, mate) for mate in mates], [whole.at[m]] * len(mates), whole.at[m]):
         copy.wait()
-    done[g] = total(whole) * scale
+    done[g] = total(whole)
     for copy in exchange(2, far, [done.at[g]] * len(far), done.at[g]):
         copy.wait()
     for k in range(groups):
         out_ref[k * rows : (k + 1) * rows, :] = done[k]
 
 
-def all_reduce(x, scale, groups, members):
+def all_reduce(x, groups, members):
     rows, cols = x.shape
     share = rows // groups
     return pl.pallas_call(
-        lambda *refs: reduce_kernel(groups, members, scale, *refs),
+        lambda *refs: reduce_kernel(groups, members, *refs),
         out_shape=jax.ShapeDtypeStruct(x.shape, x.dtype),
         in_specs=[pl.BlockSpec(memory_space=pltpu.VMEM)],
         out_specs=pl.BlockSpec(memory_space=pltpu.VMEM),
@@ -425,11 +434,19 @@
     outgoing = partials(slot, bnd_src, bnd_vals, blocks, devices)
     edge_order, edge_row, edge_col = sorted_by(grp_col, grp_row, grp_col)
     empty = in_rows < 0
-    slot_order, slot_row = sorted_by(
-        empty.astype(jnp.int32), jnp.where(empty, nb, in_rows)
-    )
+    key = jnp.where(empty, nb, in_rows)
+    slot_order, slot_row = sorted_by(key, key)
     filled = jnp.sum(~empty, dtype=jnp.int32)[None]
-    scalars = (slot_order, slot_row, filled, grp_row, grp_col, edge_order, edge_row, edge_col)
+    scalars = (
+        slot_order,
+        slot_row,
+        filled,
+        grp_row,
+        grp_col,
+        edge_order,
+        edge_row,
+        edge_col,
+    )
     outgoing, table, scalars = lax.optimization_barrier((outgoing, table, scalars))
     incoming = lax.all_to_all(
         outgoing.reshape(devices, 2 * blk, feat), AXES, split_axis=0, concat_axis=0, tiled=True
@@ -445,7 +462,9 @@
         nb,
     )
     grad_hidden = lax.psum_scatter(term, "mem", scatter_dimension=0, tiled=True)
-    grad_weight = all_reduce(local_weight, 0.5 / math.sqrt(nodes * devices), groups, members)
+    grad_weight = all_reduce(local_weight, groups, members) * (
+        0.5 / math.sqrt(nodes * devices)
+    )
     return output, grad_weight, grad_hidden.reshape(nodes, feat)
 
 

time: 357 us -> 353 us (0.989)
  transfers between devices with their start and end apart: 3 -> 3, of which waited for: 2 -> 2; matrix products, arithmetic and copies ran while one was open for 2% -> 3% of each run, Pallas kernels for 12% -> 12%
where the time goes in v5:
time: 353 us
  blocking collectives  197 us (56%)
  Pallas kernels  65.6 us (19%)
  waiting for transfers between devices  54.2 us (15%)
  between operations  14.1 us (4%)
  starting transfers between devices  11.6 us (3%)
  other arithmetic  8.9 us (3%)
    all_to_all x1, blocking collectives, per_device(): lax.all_to_all(outgoing.reshape(devices, 2 * blk, feat), AXES, split_axis...  197 us
    pallas_call x1, Pallas kernels, all_reduce(): pl.pallas_call(lambda *refs: reduce_kernel(groups, members, *refs), out_s...  32.6 us
    reduce_scatter x1, waiting for transfers between devices, per_device(): grad_hidden = lax.psum_scatter(term, 'mem', scatter_dimension=0, tiled=True)  27.6 us
    all_gather x1, waiting for transfers between devices, per_device(): table = lax.all_gather(blocks, 'mem', axis=0, tiled=True)  25.9 us
    pallas_call x1, Pallas kernels, core(): pl.pallas_call(core_kernel, in_specs=[smem] * len(scalars) + [hbm] * 5 +...  23.5 us
    all_to_all x1, starting transfers between devices, per_device(): lax.all_to_all(out_rows.reshape(devices, 2), AXES, split_axis=0, concat_a...  11.5 us
    pallas_call x1, Pallas kernels, partials(): pl.pallas_call(partial_kernel, grid_spec=pltpu.PrefetchScalarGridSpec(num...  9.44 us
  transfers between devices with their start and end apart: 3, of which 2 were waited for; matrix products, arithmetic and copies ran while one was open for 3% of the time, Pallas kernels for 12%

profile of v5, /device:TPU:1, one launch (start us, length us, event | category | flops | bytes accessed | tf_op | source)
XLA Modules:
  0.0 352.8 jit_solution(3918250833396284426)
XLA Ops:
  7.2 0.0 all-gather.2.cloned.1.call-start
  7.2 0.7 all-gather.2.cloned.1.call-update
  7.9 0.9 convert_reduce_fusion.2
  8.8 0.7 multiply_add_fusion.slot_ref
  9.5 0.0 copy-start
  9.5 0.8 select_reduce_fusion.5
  10.3 0.8 all_to_all.9
  11.0 11.5 %all-to-all-start = ((s32[128,1,2]{2,1,0:T(1,128)}), s32[128,1,2]{2,1,0:T(1,128)S(1)}, u32[]{:S(2)}, u32[]{:S(2)}) async-start(s32[128,1,2]{2,1,0:T(1,128)} %bitcast.2), calls=%async_computation | async-start | bytes 131072 | tf_op jit(solution)/shard_map/all_to_all | solution.py:430
  22.5 0.0 reduce-scatter.2.cloned.1.call-start
  22.6 0.9 convert_reduce_fusion.1
  23.5 1.5 select_reduce_fusion.2
  25.0 0.0 copy-done
  25.0 9.4 %shard_map.130 = bf16[256,128,256]{2,1,0:T(8,128)(2,1)} custom-call(s32[112]{0:T(128)} %copy-done, s32[112]{0:T(128)} %src_ref.1, bf16[112,128,128]{2,1,0:T(8,128)(2,1)} %vals_ref.1, bf16[16,128,256]{2,1,0:T(8,128)(2,1)} %bitcast.11), custom_call_target="tpu_custom_call" | custom-call | flops 939524096 | bytes 11010048 | tf_op jit(solution)/shard_map/pallas_call | solution.py:63
  34.5 0.0 all-to-all-done
  34.5 0.5 broadcast.32
  35.0 0.8 reduce.5
  35.8 0.1 reshape.65
  35.9 0.1 copy.17
  36.0 0.7 fusion.5
  36.7 0.2 convert_reduce_fusion
  36.9 0.7 select_reduce_fusion
  37.7 25.9 %all-gather.2.cloned.1.call-done.table_hbm = bf16[128,128,256]{2,1,0:T(8,128)(2,1)} async-done(((bf16[16,128,256]{2,1,0:T(8,128)(2,1)}), bf16[128,128,256]{2,1,0:T(8,128)(2,1)}) %all-gather.2.cloned.1.call-update) | async-done | bytes 8388624 | tf_op jit(solution)/shard_map/all_gather | solution.py:433
  63.6 196.9 %all_to_all.14 = bf16[128,256,256]{2,1,0:T(8,128)(2,1)} all-to-all(bf16[128,256,256]{2,1,0:T(8,128)(2,1)} %bitcast.8), channel_id=1, replica_groups=mesh['grp'=16,'mem'=8] {'grp','mem'}, dimensions={0} | all-to-all | bytes 33554432 | tf_op jit(solution)/shard_map/all_to_all | solution.py:451
  260.5 23.5 %shard_map.131 = (bf16[2048,256]{1,0:T(8,128)(2,1)}, bf16[128,128,256]{2,1,0:T(8,128)(2,1)}, f32[256,256]{1,0:T(8,128)}) custom-call(s32[256]{0:T(256)} %get-tuple-element.16.slot_order, s32[256]{0:T(256)} %get-tuple-element.17.slot_row, s32[1]{0:T(128)} %bitcast.3.filled, s32[224]{0:T(256)} %grp_row, s32[224]{0:T(256)} %grp_col, ...), custom_call_target="tpu_custom_call" | custom-call | flops 4563402752 | bytes 60000000 | tf_op jit(solution)/shard_map/pallas_call | solution.py:277
  284.0 0.0 reduce-scatter.2.cloned.1.call-update
  284.0 32.6 %shard_map.132 = f32[256,256]{1,0:T(8,128)} custom-call(f32[256,256]{1,0:T(8,128)} %get-tuple-element.27.refs_0_), custom_call_target="tpu_custom_call" | custom-call | flops 1000000 | bytes 4000000 | tf_op jit(solution)/shard_map/pallas_call | solution.py:367
  316.7 1.7 broadcast_multiply_fusion
  318.3 27.6 %reduce-scatter.2.cloned.1.call-done = bf16[16,128,256]{2,1,0:T(8,128)(2,1)} async-done(((bf16[128,128,256]{2,1,0:T(8,128)(2,1)}), bf16[16,128,256]{2,1,0:T(8,128)(2,1)}) %reduce-scatter.2.cloned.1.call-update) | async-done | bytes 1048592 | tf_op jit(solution)/shard_map/reduce_scatter | solution.py:464
  (1 shorter events, 0.0 us)
Async XLA Ops:
  7.2 56.4 %all-gather.2.cloned.1.call-start = ((), (), s32[]{:S(2)}) async-start(), calls=%async_computation.3 | async-start | bytes 9437184 | tf_op jit(solution)/shard_map/all_gather | solution.py:433
  9.5 15.5 %copy-start = (s32[112]{0:T(128)}, s32[112]{0:T(128)S(1)}, u32[]{:S(2)}) copy-start(s32[112]{0:T(128)S(1)} %multiply_add_fusion.slot_ref) | copy-start | bytes 1348
  11.0 23.4 %all-to-all-start = ((s32[128,1,2]{2,1,0:T(1,128)}), s32[128,1,2]{2,1,0:T(1,128)S(1)}, u32[]{:S(2)}, u32[]{:S(2)}) async-start(s32[128,1,2]{2,1,0:T(1,128)} %bitcast.2), calls=%async_computation | async-start | bytes 131072 | tf_op jit(solution)/shard_map/all_to_all | solution.py:430
  22.5 323.4 %reduce-scatter.2.cloned.1.call-start = ((), (), s32[]{:S(2)}) async-start(), calls=%async_computation.4 | async-start | bytes 9437184 | tf_op jit(solution)/shard_map/reduce_scatter | solution.py:464
Sparse Core Ops, SparseCore 0:
  9.7 53.7 all-gather.1
  284.1 61.7 reduce-scatter.1

commit v6 on v5

--- a/solution.py
+++ b/solution.py
@@ -268,7 +268,7 @@
 def core(scalars, incoming, table, grp_vals, initial, cotangent, weight, nb):
     count, blk, _ = grp_vals.shape
     nodes, feat = initial.shape
-    ring, chunks = 16 * BATCH, 7
+    ring, chunks = 16 * BATCH, 4
     assert count % chunks == 0 and incoming.shape[0] % BATCH == 0
     smem = pl.BlockSpec(memory_space=pltpu.SMEM)
     hbm = pl.BlockSpec(memory_space=pl.ANY)

time: 353 us -> 351 us (level)
  no operation moved by 1% of the time
where the time goes in v6:
time: 351 us; the launch traced here: 352 us
  blocking collectives  197 us (56%)
  Pallas kernels  64.5 us (18%)
  waiting for transfers between devices  54.6 us (16%)
  between operations  14.1 us (4%)
  starting transfers between devices  11.6 us (3%)
  other arithmetic  8.91 us (3%)
    all_to_all x1, blocking collectives, per_device(): lax.all_to_all(outgoing.reshape(devices, 2 * blk, feat), AXES, split_axis...  197 us
    pallas_call x1, Pallas kernels, all_reduce(): pl.pallas_call(lambda *refs: reduce_kernel(groups, members, *refs), out_s...  32.2 us
    reduce_scatter x1, waiting for transfers between devices, per_device(): grad_hidden = lax.psum_scatter(term, 'mem', scatter_dimension=0, tiled=True)  28 us
    all_gather x1, waiting for transfers between devices, per_device(): table = lax.all_gather(blocks, 'mem', axis=0, tiled=True)  25.9 us
    pallas_call x1, Pallas kernels, core(): pl.pallas_call(core_kernel, in_specs=[smem] * len(scalars) + [hbm] * 5 +...  22.8 us
    all_to_all x1, starting transfers between devices, per_device(): lax.all_to_all(out_rows.reshape(devices, 2), AXES, split_axis=0, concat_a...  11.5 us
    pallas_call x1, Pallas kernels, partials(): pl.pallas_call(partial_kernel, grid_spec=pltpu.PrefetchScalarGridSpec(num...  9.44 us
  transfers between devices with their start and end apart: 3, of which 2 were waited for; matrix products, arithmetic and copies ran while one was open for 3% of the time, Pallas kernels for 12%

profile of v6, /device:TPU:1, one launch (start us, length us, event | category | flops | bytes accessed | tf_op | source)
XLA Modules:
  0.0 352.1 jit_solution(13231618827859979802)
XLA Ops:
  7.2 0.0 all-gather.2.cloned.1.call-start
  7.2 0.7 all-gather.2.cloned.1.call-update
  7.9 0.9 convert_reduce_fusion.2
  8.8 0.7 multiply_add_fusion.slot_ref
  9.5 0.0 copy-start
  9.5 0.8 select_reduce_fusion.5
  10.3 0.8 all_to_all.9
  11.0 11.5 %all-to-all-start = ((s32[128,1,2]{2,1,0:T(1,128)}), s32[128,1,2]{2,1,0:T(1,128)S(1)}, u32[]{:S(2)}, u32[]{:S(2)}) async-start(s32[128,1,2]{2,1,0:T(1,128)} %bitcast.2), calls=%async_computation | async-start | bytes 131072 | tf_op jit(solution)/shard_map/all_to_all | solution.py:430
  22.5 0.0 reduce-scatter.2.cloned.1.call-start
  22.6 0.9 convert_reduce_fusion.1
  23.5 1.5 select_reduce_fusion.2
  25.0 0.0 copy-done
  25.0 9.4 %shard_map.130 = bf16[256,128,256]{2,1,0:T(8,128)(2,1)} custom-call(s32[112]{0:T(128)} %copy-done, s32[112]{0:T(128)} %src_ref.1, bf16[112,128,128]{2,1,0:T(8,128)(2,1)} %vals_ref.1, bf16[16,128,256]{2,1,0:T(8,128)(2,1)} %bitcast.11), custom_call_target="tpu_custom_call" | custom-call | flops 939524096 | bytes 11010048 | tf_op jit(solution)/shard_map/pallas_call | solution.py:63
  34.5 0.0 all-to-all-done
  34.5 0.5 broadcast.32
  35.0 0.8 reduce.5
  35.8 0.1 reshape.65
  35.9 0.1 copy.17
  36.0 0.7 fusion.5
  36.7 0.2 convert_reduce_fusion
  36.9 0.7 select_reduce_fusion
  37.7 25.9 %all-gather.2.cloned.1.call-done.table_hbm = bf16[128,128,256]{2,1,0:T(8,128)(2,1)} async-done(((bf16[16,128,256]{2,1,0:T(8,128)(2,1)}), bf16[128,128,256]{2,1,0:T(8,128)(2,1)}) %all-gather.2.cloned.1.call-update) | async-done | bytes 8388624 | tf_op jit(solution)/shard_map/all_gather | solution.py:433
  63.6 196.9 %all_to_all.14 = bf16[128,256,256]{2,1,0:T(8,128)(2,1)} all-to-all(bf16[128,256,256]{2,1,0:T(8,128)(2,1)} %bitcast.8), channel_id=1, replica_groups=mesh['grp'=16,'mem'=8] {'grp','mem'}, dimensions={0} | all-to-all | bytes 33554432 | tf_op jit(solution)/shard_map/all_to_all | solution.py:451
  260.5 22.8 %shard_map.131 = (bf16[2048,256]{1,0:T(8,128)(2,1)}, bf16[128,128,256]{2,1,0:T(8,128)(2,1)}, f32[256,256]{1,0:T(8,128)}) custom-call(s32[256]{0:T(256)} %get-tuple-element.16.slot_order, s32[256]{0:T(256)} %get-tuple-element.17.slot_row, s32[1]{0:T(128)} %bitcast.3.filled, s32[224]{0:T(256)} %grp_row, s32[224]{0:T(256)} %grp_col, ...), custom_call_target="tpu_custom_call" | custom-call | flops 4563402752 | bytes 60000000 | tf_op jit(solution)/shard_map/pallas_call | solution.py:277
  283.3 0.0 reduce-scatter.2.cloned.1.call-update
  283.3 32.2 %shard_map.132 = f32[256,256]{1,0:T(8,128)} custom-call(f32[256,256]{1,0:T(8,128)} %get-tuple-element.27.refs_0_), custom_call_target="tpu_custom_call" | custom-call | flops 1000000 | bytes 4000000 | tf_op jit(solution)/shard_map/pallas_call | solution.py:367
  315.6 1.7 broadcast_multiply_fusion
  317.2 28.0 %reduce-scatter.2.cloned.1.call-done = bf16[16,128,256]{2,1,0:T(8,128)(2,1)} async-done(((bf16[128,128,256]{2,1,0:T(8,128)(2,1)}), bf16[16,128,256]{2,1,0:T(8,128)(2,1)}) %reduce-scatter.2.cloned.1.call-update) | async-done | bytes 1048592 | tf_op jit(solution)/shard_map/reduce_scatter | solution.py:464
  (1 shorter events, 0.0 us)
Async XLA Ops:
  7.2 56.4 %all-gather.2.cloned.1.call-start = ((), (), s32[]{:S(2)}) async-start(), calls=%async_computation.3 | async-start | bytes 9437184 | tf_op jit(solution)/shard_map/all_gather | solution.py:433
  9.5 15.5 %copy-start = (s32[112]{0:T(128)}, s32[112]{0:T(128)S(1)}, u32[]{:S(2)}) copy-start(s32[112]{0:T(128)S(1)} %multiply_add_fusion.slot_ref) | copy-start | bytes 1348
  11.0 23.4 %all-to-all-start = ((s32[128,1,2]{2,1,0:T(1,128)}), s32[128,1,2]{2,1,0:T(1,128)S(1)}, u32[]{:S(2)}, u32[]{:S(2)}) async-start(s32[128,1,2]{2,1,0:T(1,128)} %bitcast.2), calls=%async_computation | async-start | bytes 131072 | tf_op jit(solution)/shard_map/all_to_all | solution.py:430
  22.5 322.7 %reduce-scatter.2.cloned.1.call-start = ((), (), s32[]{:S(2)}) async-start(), calls=%async_computation.4 | async-start | bytes 9437184 | tf_op jit(solution)/shard_map/reduce_scatter | solution.py:464
Sparse Core Ops, SparseCore 0:
  9.7 53.7 all-gather.1
  283.4 61.7 reduce-scatter.1
